TPU v7x, 256 devices: a whole 4x4x8 slice. The times are simulated.
256 devices in a mesh: term: 64 (over z, x, core), sector: 4 (over y).
Axes of the slice: x: 4, y: 4, z: 8, core: 2. Of those that a mesh axis runs over, the one named last changes fastest.
Arguments:
- psi_start: float32 [4, 384, 384], P('sector'), may hold values from -6 to 6
- diagonal: float32 [4, 384, 384], P('sector'), may hold values from -3 to 3
- left_ops: float32 [1024, 384, 384], P(('term', 'sector')), may hold values from -0.3125 to 0.3125
- right_ops: float32 [1024, 384, 384], P(('term', 'sector')), may hold values from -0.02734375 to 0.02734375
- pair_in: int32 [256, 4], P(('term', 'sector')), may hold values from 0 to 3
- pair_out: int32 [256, 4], P(('term', 'sector')), may hold values from 0 to 3
- pair_count: int32 [256], P(('term', 'sector')), may hold values from 1 to 4, as said below
Outputs:
- psi_final: float32 [4, 384, 384], P('sector')
- energies: float32 [2], replicated
Inputs may be any that keep to these rules, and one draw needn't show every extreme that they name: `pair_count`: some device has all 4 slots live in every draw.
All inputs are finite; a program needn't handle non-finite values.
Results may differ from a plain program's by a relative error of at most 0.00013.
Values sent between devices are 32-bit elements; how exact they have to be, the bound alone decides.
A program may use at most 64 MiB of HBM per device.

v0:
```python
import functools

import jax
import jax.numpy as jnp
from jax import lax
from jax.sharding import Mesh
from jax.sharding import PartitionSpec as P

ITERS = 2
TERM = ("term_0", "term_1", "term_2")
TERM_SECTOR = ("term_0", "term_1", "term_2", "sector")


epsilon = 1e-06


def over_axes(array, axes):
    return functools.reduce(lax.psum, axes, array)


def copy_for_each(array, axis):
    copies = jnp.broadcast_to(array, (lax.axis_size(axis), *array.shape))
    return lax.all_to_all(copies, axis, split_axis=0, concat_axis=0, tiled=True)


def joined_along(pieces, dim):
    lengths = list(pieces.shape[1:])
    lengths[dim] *= pieces.shape[0]
    return jnp.moveaxis(pieces, 0, dim).reshape(lengths)


def gather_directly(array, axis, dim):
    pieces = copy_for_each(array, axis)
    return joined_along(pieces, dim)


def split_up(array, dim, peers):
    lengths = array.shape
    pieces = array.reshape(*lengths[:dim], peers, lengths[dim] // peers, *lengths[dim + 1 :])
    return jnp.moveaxis(pieces, dim, 0)


def sent_and_summed(array, axis, dim):
    pieces = split_up(array, dim, lax.axis_size(axis))
    arrived = lax.all_to_all(pieces, axis, split_axis=0, concat_axis=0, tiled=True)
    return arrived.sum(axis=0)


def apply_pairs(gathered, left_ops, right_ops, pair_in, pair_out, pair_count):

    def one_pair(pair_slot, partial_value):
        source = lax.dynamic_index_in_dim(gathered, pair_in[0, pair_slot], 0, keepdims=False)
        left_block = lax.dynamic_index_in_dim(left_ops, pair_slot, 0, keepdims=False)
        right_block = lax.dynamic_index_in_dim(right_ops, pair_slot, 0, keepdims=False)
        inner_prod = jnp.dot(left_block, source, precision=lax.Precision.HIGHEST)
        product = lax.dot_general(
            inner_prod, right_block, (((1,), (1,)), ((), ())), precision=lax.Precision.HIGHEST
        )
        target = pair_out[0, pair_slot]
        current = lax.dynamic_index_in_dim(partial_value, target, 0, keepdims=False)
        return lax.dynamic_update_index_in_dim(partial_value, current + product, target, 0)

    return lax.fori_loop(0, pair_count[0], one_pair, jnp.zeros(gathered.shape, jnp.float32))


def row_share(array):
    row_count = array.shape[1] // lax.axis_size(TERM)
    return lax.dynamic_slice_in_dim(array, lax.axis_index(TERM) * row_count, row_count, 1)


def global_sums(values):
    return (over_axes(values[0], TERM_SECTOR),)


def sigma_blocks(vector, left_ops, right_ops, pair_in, pair_out, pair_count):
    gathered = gather_directly(vector, "sector", 0)
    partial_value = apply_pairs(gathered, left_ops, right_ops, pair_in, pair_out, pair_count)
    owned_sum = sent_and_summed(partial_value, "sector", 0)
    return sent_and_summed(owned_sum, TERM, 1)


def shards(psi_start, diagonal, left_ops, right_ops, pair_in, pair_out, pair_count):
    vector = psi_start
    cell_total = float(
        psi_start.shape[0] * lax.axis_size("sector") * psi_start.shape[1] * psi_start.shape[2]
    )
    diag_share = row_share(diagonal)
    energies = []
    for sweep in range(ITERS):
        vec_share = row_share(vector)
        squares = global_sums((jnp.sum(vec_share * vec_share),))[0]
        inverse_norm = 1.0 / jnp.sqrt(squares / cell_total + epsilon)
        normed = vector * inverse_norm
        sigma = sigma_blocks(normed, left_ops, right_ops, pair_in, pair_out, pair_count)
        normed_share = row_share(normed)
        product_sum = global_sums((jnp.sum(normed_share * sigma),))[0]
        rayleigh = product_sum / cell_total
        residual = sigma - rayleigh * normed_share
        correction = residual / jnp.maximum(jnp.abs(diag_share - rayleigh), 1.0)
        updated = normed_share - correction
        vector = gather_directly(updated, TERM, 1)
        energies.append(rayleigh)
    return (vector, jnp.stack(energies))


def solution(mesh):
    finer = Mesh(
        mesh.devices.reshape(8, 4, 2, mesh.shape["sector"]),
        ("term_0", "term_1", "term_2", "sector"),
    )
    in_specs = (
        P("sector", None, None),
        P("sector", None, None),
        P(TERM_SECTOR, None, None),
        P(TERM_SECTOR, None, None),
        P(TERM_SECTOR, None),
        P(TERM_SECTOR, None),
        P(TERM_SECTOR),
    )
    out_specs = (P("sector", None, None), P())
    return jax.shard_map(
        shards, mesh=finer, in_specs=in_specs, out_specs=out_specs, check_vma=False
    )
```

profile of v0, /device:TPU:1, one launch (start us, length us, event | category | flops | bytes accessed | tf_op | source)
XLA Modules:
  0.0 499.5 jit_solution(1539146294675107279)
XLA Ops:
  0.7 1.4 multiply_reduce_fusion.1
  2.1 17.9 %psum.112 = f32[]{:T(128)} all-reduce(f32[]{:T(128)} %multiply_reduce_fusion.1), channel_id=1, replica_groups=mesh['term_0'=8,'term_1'=4,'term_2'=2,'sector'=4] {'term_0'}, use_global_device_ids=true, to_apply=%region_1.0 | all-reduce | flops 1 | bytes 8 | tf_op jit(solution)/shard_map/psum | solution.py:18
  20.0 9.1 %psum.113 = f32[]{:T(128)} all-reduce(f32[]{:T(128)} %psum.112), channel_id=1, replica_groups=mesh['term_0'=8,'term_1'=4,'term_2'=2,'sector'=4] {'term_1'}, use_global_device_ids=true, to_apply=%region_2.0 | all-reduce | flops 1 | bytes 8 | tf_op jit(solution)/shard_map/psum | solution.py:18
  29.1 9.0 %psum.114 = f32[]{:T(128)} all-reduce(f32[]{:T(128)} %psum.113), channel_id=1, replica_groups=mesh['term_0'=8,'term_1'=4,'term_2'=2,'sector'=4] {'term_2'}, use_global_device_ids=true, to_apply=%region_3.0 | all-reduce | flops 1 | bytes 8 | tf_op jit(solution)/shard_map/psum | solution.py:18
  38.0 9.3 %psum.115 = f32[]{:T(128)} all-reduce(f32[]{:T(128)} %psum.114), channel_id=1, replica_groups=mesh['term_0'=8,'term_1'=4,'term_2'=2,'sector'=4] {'sector'}, use_global_device_ids=true, to_apply=%region_4.0 | all-reduce | flops 1 | bytes 8 | tf_op jit(solution)/shard_map/psum | solution.py:18
  48.0 1.7 copy_multiply_fusion
  50.6 1.6 broadcast_in_dim.19
  52.1 3.6 all-to-all-start
  55.8 26.8 %all-to-all-done = f32[4,1,384,384]{3,2,1,0:T(8,128)S(1)} async-done(((f32[4,1,384,384]{3,2,1,0:T(8,128)}), f32[4,1,384,384]{3,2,1,0:T(8,128)S(1)}, u32[]{:S(2)}, u32[]{:S(2)}) %all-to-all-start) | async-done | bytes 2359328 | tf_op jit(solution)/shard_map/all_to_all | solution.py:23
  82.6 1.4 copy-done.2
  84.1 21.4 %while.20 = (s32[]{:T(128)}, f32[4,384,384]{2,1,0:T(8,128)S(1)}, s32[]{:T(128)}, s32[1,4]{1,0:T(1,128)S(1)}, f32[4,384,384]{2,1,0:T(8,128)}, /*index=5*/s32[1,4]...) while((s32[]{:T(128)}, f32[4,384,384]{2,1,0:T(8,128)S(1)}, ...), condition=%wide.region_6.7_spmd, body=%wide.region_5.6_spmd.sunk | while | flops 1359101952 | bytes 5308667 | solution.py:63
  87.7 2.5 fusion.40
  92.2 2.3 fusion.41
  98.1 2.5 fusion.40
  102.6 2.3 fusion.41
  105.6 39.6 %all_to_all.41 = f32[4,1,384,384]{3,2,1,0:T(8,128)} all-to-all(f32[4,1,384,384]{3,2,1,0:T(8,128)S(1)} %bitcast.86), channel_id=1, replica_groups=mesh['term_0'=8,'term_1'=4,'term_2'=2,'sector'=4] {'sector'}, dimensions={0} | all-to-all | bytes 4718592 | tf_op jit(solution)/shard_map/all_to_all | solution.py:45
  145.2 1.9 reduce_sum.77
  147.6 37.8 %all_to_all.42 = f32[64,1,6,384]{3,1,2,0:T(1,128)S(1)} all-to-all(f32[64,1,6,384]{3,1,2,0:T(1,128)S(1)} %transpose_reshape.8), channel_id=1, replica_groups=mesh['term_0'=8,'term_1'=4,'term_2'=2,'sector'=4] {'term_0','term_1','te..., dimensions={0} | all-to-all | bytes 1179648 | tf_op jit(solution)/shard_map/all_to_all | solution.py:45
  185.8 1.3 multiply_reduce_fusion.4
  187.1 12.8 %psum.116 = f32[]{:T(128)} all-reduce(f32[]{:T(128)} %multiply_reduce_fusion.4), channel_id=1, replica_groups=mesh['term_0'=8,'term_1'=4,'term_2'=2,'sector'=4] {'term_0'}, use_global_device_ids=true, to_apply=%region_10.11 | all-reduce | flops 1 | bytes 8 | tf_op jit(solution)/shard_map/psum | solution.py:18
  199.9 7.7 %psum.117 = f32[]{:T(128)} all-reduce(f32[]{:T(128)} %psum.116), channel_id=1, replica_groups=mesh['term_0'=8,'term_1'=4,'term_2'=2,'sector'=4] {'term_1'}, use_global_device_ids=true, to_apply=%region_11.12 | all-reduce | flops 1 | bytes 8 | tf_op jit(solution)/shard_map/psum | solution.py:18
  207.6 9.3 %psum.118 = f32[]{:T(128)} all-reduce(f32[]{:T(128)} %psum.117), channel_id=1, replica_groups=mesh['term_0'=8,'term_1'=4,'term_2'=2,'sector'=4] {'term_2'}, use_global_device_ids=true, to_apply=%region_12.13 | all-reduce | flops 1 | bytes 8 | tf_op jit(solution)/shard_map/psum | solution.py:18
  216.9 7.5 %psum.119 = f32[]{:T(128)} all-reduce(f32[]{:T(128)} %psum.118), channel_id=1, replica_groups=mesh['term_0'=8,'term_1'=4,'term_2'=2,'sector'=4] {'sector'}, use_global_device_ids=true, to_apply=%region_13.14 | all-reduce | flops 1 | bytes 8 | tf_op jit(solution)/shard_map/psum | solution.py:18
  226.2 26.5 %all_to_all.40 = f32[64,1,6,384]{3,1,2,0:T(1,128)S(1)} all-to-all(f32[64,1,6,384]{3,1,2,0:T(1,128)S(1)} %broadcast_in_dim.20), channel_id=1, replica_groups=mesh['term_0'=8,'term_1'=4,'term_2'=2,'sector'=4] {'term_0','term_1','te..., dimensions={0} | all-to-all | bytes 1179648 | tf_op jit(solution)/shard_map/all_to_all | solution.py:23
  253.4 12.8 %psum.120 = f32[]{:T(128)} all-reduce(f32[]{:T(128)} %multiply_reduce_fusion.3), channel_id=1, replica_groups=mesh['term_0'=8,'term_1'=4,'term_2'=2,'sector'=4] {'term_0'}, use_global_device_ids=true, to_apply=%region_15.16 | all-reduce | flops 1 | bytes 8 | tf_op jit(solution)/shard_map/psum | solution.py:18
  266.2 7.7 %psum.121 = f32[]{:T(128)} all-reduce(f32[]{:T(128)} %psum.120), channel_id=1, replica_groups=mesh['term_0'=8,'term_1'=4,'term_2'=2,'sector'=4] {'term_1'}, use_global_device_ids=true, to_apply=%region_16.17 | all-reduce | flops 1 | bytes 8 | tf_op jit(solution)/shard_map/psum | solution.py:18
  273.9 9.3 %psum.122 = f32[]{:T(128)} all-reduce(f32[]{:T(128)} %psum.121), channel_id=1, replica_groups=mesh['term_0'=8,'term_1'=4,'term_2'=2,'sector'=4] {'term_2'}, use_global_device_ids=true, to_apply=%region_17.18 | all-reduce | flops 1 | bytes 8 | tf_op jit(solution)/shard_map/psum | solution.py:18
  283.2 7.2 %psum.123 = f32[]{:T(128)} all-reduce(f32[]{:T(128)} %psum.122), channel_id=1, replica_groups=mesh['term_0'=8,'term_1'=4,'term_2'=2,'sector'=4] {'sector'}, use_global_device_ids=true, to_apply=%region_18.19 | all-reduce | flops 1 | bytes 8 | tf_op jit(solution)/shard_map/psum | solution.py:18
  291.1 1.6 multiply_reduce_fusion
  292.8 1.6 broadcast_in_dim.21
  294.3 3.6 all-to-all-start.4
  298.0 26.8 %all-to-all-done.4 = f32[4,1,384,384]{3,2,1,0:T(8,128)S(1)} async-done(((f32[4,1,384,384]{3,2,1,0:T(8,128)}), f32[4,1,384,384]{3,2,1,0:T(8,128)S(1)}, u32[]{:S(2)}, u32[]{:S(2)}) %all-to-all-start.4) | async-done | bytes 2359328 | tf_op jit(solution)/shard_map/all_to_all | solution.py:23
  324.8 1.4 copy-done.1
  326.3 22.5 %while.21 = (s32[]{:T(128)}, f32[4,384,384]{2,1,0:T(8,128)S(1)}, s32[]{:T(128)}, s32[1,4]{1,0:T(1,128)S(1)}, f32[4,384,384]{2,1,0:T(8,128)}, /*index=5*/s32[1,4]...) while((s32[]{:T(128)}, f32[4,384,384]{2,1,0:T(8,128)S(1)}, ...), condition=%wide.region_20.21_spmd, body=%wide.region_19.20_spmd.sunk | while | flops 1359101952 | bytes 5308667 | solution.py:63
  330.4 2.5 fusion.46
  335.0 2.3 fusion.47
  341.2 2.5 fusion.46
  345.8 2.3 fusion.47
  348.8 40.5 %all_to_all.43 = f32[4,1,384,384]{3,2,1,0:T(8,128)} all-to-all(f32[4,1,384,384]{3,2,1,0:T(8,128)S(1)} %bitcast.87), channel_id=1, replica_groups=mesh['term_0'=8,'term_1'=4,'term_2'=2,'sector'=4] {'sector'}, dimensions={0} | all-to-all | bytes 4718592 | tf_op jit(solution)/shard_map/all_to_all | solution.py:45
  389.3 1.9 reduce_sum.82
  391.7 38.7 %all_to_all.44 = f32[64,1,6,384]{3,1,2,0:T(1,128)S(1)} all-to-all(f32[64,1,6,384]{3,1,2,0:T(1,128)S(1)} %transpose_reshape.9), channel_id=1, replica_groups=mesh['term_0'=8,'term_1'=4,'term_2'=2,'sector'=4] {'term_0','term_1','te..., dimensions={0} | all-to-all | bytes 1179648 | tf_op jit(solution)/shard_map/all_to_all | solution.py:45
  430.8 1.3 multiply_reduce_fusion.2
  432.1 12.8 %psum.124 = f32[]{:T(128)} all-reduce(f32[]{:T(128)} %multiply_reduce_fusion.2), channel_id=1, replica_groups=mesh['term_0'=8,'term_1'=4,'term_2'=2,'sector'=4] {'term_0'}, use_global_device_ids=true, to_apply=%region_24.25 | all-reduce | flops 1 | bytes 8 | tf_op jit(solution)/shard_map/psum | solution.py:18
  444.9 7.7 %psum.125 = f32[]{:T(128)} all-reduce(f32[]{:T(128)} %psum.124), channel_id=1, replica_groups=mesh['term_0'=8,'term_1'=4,'term_2'=2,'sector'=4] {'term_1'}, use_global_device_ids=true, to_apply=%region_25.26 | all-reduce | flops 1 | bytes 8 | tf_op jit(solution)/shard_map/psum | solution.py:18
  452.6 9.3 %psum.126 = f32[]{:T(128)} all-reduce(f32[]{:T(128)} %psum.125), channel_id=1, replica_groups=mesh['term_0'=8,'term_1'=4,'term_2'=2,'sector'=4] {'term_2'}, use_global_device_ids=true, to_apply=%region_26.27 | all-reduce | flops 1 | bytes 8 | tf_op jit(solution)/shard_map/psum | solution.py:18
  461.9 7.5 %psum.127 = f32[]{:T(128)} all-reduce(f32[]{:T(128)} %psum.126), channel_id=1, replica_groups=mesh['term_0'=8,'term_1'=4,'term_2'=2,'sector'=4] {'sector'}, use_global_device_ids=true, to_apply=%region_27.28 | all-reduce | flops 1 | bytes 8 | tf_op jit(solution)/shard_map/psum | solution.py:18
  471.9 7.7 %all-to-all-start.7 = ((f32[64,1,6,384]{3,1,2,0:T(1,128)}), f32[64,1,6,384]{3,1,2,0:T(1,128)S(1)}, u32[]{:S(2)}, u32[]{:S(2)}) async-start(f32[64,1,6,384]{3,1,2,0:T(1,128)} %broadcast_in_dim.22), calls=%async_computation.7 | async-start | bytes 1179648 | tf_op jit(solution)/shard_map/all_to_all | solution.py:23
  480.2 18.5 %all-to-all-done.7 = f32[64,1,6,384]{3,1,2,0:T(1,128)S(1)} async-done(((f32[64,1,6,384]{3,1,2,0:T(1,128)}), f32[64,1,6,384]{3,1,2,0:T(1,128)S(1)}, u32[]{:S(2)}, u32[]{:S(2)}) %all-to-all-start.7) | async-done | bytes 589856 | tf_op jit(solution)/shard_map/all_to_all | solution.py:23
  (36 shorter events, 13.5 us)
Async XLA Ops:
  0.6 216.3 %copy-start = (f32[1,384,384]{2,1,0:T(8,128)S(1)}, f32[1,384,384]{2,1,0:T(8,128)}, u32[]{:S(2)}) copy-start(f32[1,384,384]{2,1,0:T(8,128)} %param.12) | copy-start | bytes 1769476
  49.7 0.8 copy-start.4
  52.1 30.4 %all-to-all-start = ((f32[4,1,384,384]{3,2,1,0:T(8,128)}), f32[4,1,384,384]{3,2,1,0:T(8,128)S(1)}, u32[]{:S(2)}, u32[]{:S(2)}) async-start(f32[4,1,384,384]{3,2,1,0:T(8,128)} %broadcast_in_dim.19), calls=%async_computation | async-start | bytes 4718592 | tf_op jit(solution)/shard_map/all_to_all | solution.py:23
  55.8 28.3 %copy-start.5 = (s32[1,4]{1,0:T(1,128)S(1)}, s32[1,4]{1,0:T(1,128)}, u32[]{:S(2)}) copy-start(s32[1,4]{1,0:T(1,128)} %param.16) | copy-start | bytes 52
  82.6 1.4 copy-start.2
  252.7 41.7 %copy-start.3 = (f32[64,1,6,384]{3,1,2,0:T(1,128)}, f32[64,1,6,384]{3,1,2,0:T(1,128)S(1)}, u32[]{:S(2)}) copy-start(f32[64,1,6,384]{3,1,2,0:T(1,128)S(1)} %all_to_all.40) | copy-start | bytes 1769476
  294.3 30.4 %all-to-all-start.4 = ((f32[4,1,384,384]{3,2,1,0:T(8,128)}), f32[4,1,384,384]{3,2,1,0:T(8,128)S(1)}, u32[]{:S(2)}, u32[]{:S(2)}) async-start(f32[4,1,384,384]{3,2,1,0:T(8,128)} %broadcast_in_dim.21), calls=%async_computation.4 | async-start | bytes 4718592 | tf_op jit(solution)/shard_map/all_to_all | solution.py:23
  324.8 1.4 copy-start.1
  471.9 26.7 %all-to-all-start.7 = ((f32[64,1,6,384]{3,1,2,0:T(1,128)}), f32[64,1,6,384]{3,1,2,0:T(1,128)S(1)}, u32[]{:S(2)}, u32[]{:S(2)}) async-start(f32[64,1,6,384]{3,1,2,0:T(1,128)} %broadcast_in_dim.22), calls=%async_computation.7 | async-start | bytes 1179648 | tf_op jit(solution)/shard_map/all_to_all | solution.py:23
where the time goes:
time: 501 us; the launch traced here: 500 us
  blocking collectives  340 us (68%)
  waiting for transfers between devices  72 us (14%)
  matrix products  19.3 us (4%)
  loops' own time  19.2 us (4%)
  local copies, waits for them, and re-layouts  16 us (3%)
  starting transfers between devices  14.9 us (3%)
  other arithmetic  14.5 us (3%)
    psum x16, blocking collectives, over_axes(): return functools.reduce(lax.psum, axes, array)  157 us
    all_to_all x4, blocking collectives, sent_and_summed(): lax.all_to_all(pieces, axis, split_axis=0, concat_axis=0, tiled=True)  157 us
    all_to_all x3, waiting for transfers between devices, copy_for_each(): return lax.all_to_all(copies, axis, split_axis=0, concat_axis=0, tiled=True)  72 us
    all_to_all x1, blocking collectives, copy_for_each(): return lax.all_to_all(copies, axis, split_axis=0, concat_axis=0, tiled=True)  26.5 us
    another operation x2, loops' own time, apply_pairs(): lax.fori_loop(0, pair_count[0], one_pair, jnp.zeros(gathered.shape, jnp.f...  19.2 us
    all_to_all x3, starting transfers between devices, copy_for_each(): return lax.all_to_all(copies, axis, split_axis=0, concat_axis=0, tiled=True)  14.9 us
    dot_general x4, matrix products, one_pair(): inner_prod = jnp.dot(left_block, source, precision=lax.Precision.HIGHEST)  10 us
  transfers between devices with their start and end apart: 3, of which 3 were waited for; matrix products, arithmetic and copies ran while one was open for 0% of the time, Pallas kernels for 0%

commit v1 on v0

v1 whole, which is shorter than its diff:
```python
import functools

import jax
import jax.numpy as jnp
from jax import lax
from jax.experimental import pallas as pl
from jax.experimental.pallas import tpu as pltpu
from jax.sharding import PartitionSpec as P

STEPS = 2
EPSILON = 1e-06
N = 384
CELLS = float(4 * N * N)
F32 = jnp.float32
BF16 = jnp.bfloat16


def matmul(a, b):
    return lax.dot_general(a, b, (((1,), (0,)), ((), ())), preferred_element_type=F32)


def halves(value):
    high = value.astype(BF16)
    return high, (value - high.astype(F32)).astype(BF16)


def kernel(
    pair_in,
    pair_out,
    pair_count,
    psi,
    diagonal,
    left_hbm,
    right_hbm,
    out,
    energies,
    left,
    right,
    left3,
    right3,
    vec3,
    inner3,
    product,
    vecs,
    part_far,
    part_near,
    core_in,
    big_in,
    mid,
    small_in,
    last,
    z_in,
    fresh,
    dots_c,
    dots_x,
    dots_y,
    dots_z,
    load_sem,
    init_s,
    init_r,
    init_cs,
    init_cr,
    core_s,
    core_r,
    big_s,
    big_r,
    small_s,
    small_r,
    z_s,
    z_r,
    zg_s,
    zg_r,
    sg_s,
    sg_r,
    bg_s,
    bg_r,
    cg_s,
    cg_r,
    dot_s,
    dot_r,
):
    t = lax.axis_index("term")
    y = lax.axis_index("sector")
    z = t // 8
    x = lax.rem(t // 2, 4)
    c = lax.rem(t, 2)
    d = 1 - c

    def device(z_, x_, c_, y_):
        return ((z_ * 4 + x_) * 2 + c_, y_)

    def x_to(k):
        return device(z, lax.rem(x + k, 4), c, y)

    def y_to(k):
        return device(z, x, c, lax.rem(y + k, 4))

    def z_to(k):
        return device(lax.rem(z + k, 8), x, c, y)

    sibling = device(z, x, d, y)

    loads = []
    for index, (source, target) in enumerate(((right_hbm, right), (left_hbm, left))):
        load = pltpu.make_async_copy(source, target, load_sem.at[index])
        load.start()
        loads.append(load)

    barrier = pltpu.get_barrier_semaphore()
    peers = [sibling]
    peers += [x_to(k) for k in (1, 2, 3)]
    peers += [y_to(k) for k in (1, 2, 3)]
    peers += [z_to(k) for k in range(1, 8)]
    for peer in peers:
        pl.semaphore_signal(barrier, inc=1, device_id=peer, device_id_type=pl.DeviceIdType.MESH)

    sent = []

    def send(source, target, send_sem, recv_sem, peer):
        copy = pltpu.make_async_remote_copy(
            src_ref=source,
            dst_ref=target,
            send_sem=send_sem,
            recv_sem=recv_sem,
            device_id=peer,
            device_id_type=pl.DeviceIdType.MESH,
        )
        copy.start()
        sent.append(copy)
        return copy

    first = vecs.at[0]
    for cc in range(2):
        for xx in range(4):
            row = 96 * xx + 48 * cc
            first[cc, 0, xx, y] = psi[0, row : row + 24].reshape(3, 8, N)
            first[cc, 1, y, xx] = psi[0, row + 24 : row + 48].reshape(3, 8, N)

    pl.semaphore_wait(barrier, len(peers))

    near = []
    whole = []
    for k in (1, 2, 3):
        here = first.at[c, 0, x, y]
        near.append(send(here, here, init_s.at[0, k - 1], init_r.at[0, k - 1], y_to(k)))
    for k in (1, 2, 3):
        here = first.at[c, 1, y]
        whole.append(send(here, here, init_s.at[1, k - 1], init_r.at[1, k - 1], y_to(k)))

    loads[0].wait()

    def split_right(j, carry):
        high, low = halves(right[j].T)
        right3[j, 0:N] = high
        right3[j, N : 2 * N] = high
        right3[j, 2 * N :] = low
        return carry

    lax.fori_loop(0, 4, split_right, 0)

    forward = {}
    crossing = []
    for k in (1, 2, 3):
        near[k - 1].wait_recv()
        from_y = lax.rem(y + 4 - k, 4)
        here = first.at[c, 0, x, from_y]
        for m in (1, 2, 3):
            forward[k, m] = send(
                here, here, init_s.at[1 + k, m - 1], init_r.at[1 + k, m - 1], x_to(m)
            )
        crossing.append(send(here, here, init_cs.at[k - 1, 0], init_cr.at[k - 1, 0], sibling))

    loads[1].wait()

    def split_left(j, carry):
        for cc in range(2):
            for xx in range(4):
                row = 96 * xx + 48 * cc
                high, low = halves(left[j, row : row + 48])
                rows = slice(48 * xx, 48 * xx + 48)
                left3[j, cc, rows, 0:N] = high
                left3[j, cc, rows, N : 2 * N] = high
                left3[j, cc, rows, 2 * N :] = low
        return carry

    lax.fori_loop(0, 4, split_left, 0)

    for k in (1, 2, 3):
        whole[k - 1].wait_recv()
        here = first.at[c, 1, lax.rem(y + 4 - k, 4)]
        crossing.append(send(here, here, init_cs.at[k - 1, 4], init_cr.at[k - 1, 4], sibling))
    for k in (1, 2, 3):
        for m in (1, 2, 3):
            forward[k, m].wait_recv()
            here = first.at[c, 0, lax.rem(x + 4 - m, 4), lax.rem(y + 4 - k, 4)]
            crossing.append(send(here, here, init_cs.at[k - 1, m], init_cr.at[k - 1, m], sibling))
    for copy in crossing:
        copy.wait_recv()

    row0 = pl.multiple_of(96 * x + 48 * c + 8 * z, 8)
    for step in range(STEPS):
        vec = vecs.at[step]

        def convert(index, total):
            yy, xx = index // 4, lax.rem(index, 4)
            for cc in range(2):
                top = vec[cc, 0, xx, yy].reshape(24, N)
                low_rows = vec[cc, 1, yy, xx].reshape(24, N)
                block = jnp.concatenate([top, low_rows], axis=0)
                total = total + jnp.sum((block * block).reshape(6, 8, N), axis=0)
                high, low = halves(block)
                rows = pl.ds(pl.multiple_of(96 * xx + 48 * cc, 16), 48)
                vec3[yy, rows, 0:N] = high
                vec3[yy, rows, N : 2 * N] = low
                vec3[yy, rows, 2 * N :] = high
            return total

        squares = lax.fori_loop(0, 16, convert, jnp.zeros((8, N), F32))
        mean_square = jnp.sum(squares, axis=(0, 1), keepdims=True) / CELLS + EPSILON
        inverse = 1.0 / jnp.sqrt(mean_square)

        for j in range(4):
            high, low = halves(matmul(vec3[pair_in[0, j]], right3[j]))
            inner3[j, 0:N] = high
            inner3[j, N : 2 * N] = low
            inner3[j, 2 * N :] = high

        count = pair_count[0]
        chosen = [
            [jnp.logical_and(pair_out[0, j] == yy, count > j) for yy in range(4)] for j in range(4)
        ]

        def products(side, target):
            for j in range(4):
                product[j] = matmul(left3[j, side], inner3[j])

            def combine(xx, total):
                for cls in range(2):
                    rows = pl.ds(pl.multiple_of(48 * xx + 24 * cls, 8), 24)
                    blocks = [product[j, rows].reshape(3, 8, N) for j in range(4)]
                    for yy in range(4):
                        p, q = (xx, yy) if cls == 0 else (yy, xx)
                        value = jnp.where(chosen[0][yy], blocks[0], 0.0)
                        for j in range(1, 4):
                            value = value + jnp.where(chosen[j][yy], blocks[j], 0.0)
                        target[cls, p, q] = value
                        total = total + jnp.sum(value * vec[side, cls, p, q], axis=0)
                return total

            return lax.fori_loop(0, 4, combine, jnp.zeros((8, N), F32))

        far, own = part_far.at[step], part_near.at[step]
        dot = products(d, far)
        core = send(far, core_in.at[step], core_s.at[step], core_r.at[step], sibling)
        dot = dot + products(c, own)
        dots_c[step, c] = dot[:, 0:128] + dot[:, 128:256] + dot[:, 256:384]
        here = dots_c.at[step, c]
        dot_copies = [send(here, here, dot_s.at[step, 0], dot_r.at[step, 0], sibling)]

        core.wait_recv()
        big = []
        for k in (1, 2, 3, 0):
            for cls in range(2):
                p = lax.rem((x if cls == 0 else y) + k, 4)
                own[cls, p] = own[cls, p] + core_in[step, cls, p]
                if k:
                    big.append(
                        send(
                            own.at[cls, p],
                            big_in.at[step, cls, k - 1],
                            big_s.at[step, cls, k - 1],
                            big_r.at[step, cls, k - 1],
                            (x_to if cls == 0 else y_to)(k),
                        )
                    )
        dot_copies[0].wait_recv()
        dots_x[step, x] = dots_c[step, 0] + dots_c[step, 1]
        here = dots_x.at[step, x]
        dot_copies = [
            send(here, here, dot_s.at[step, k], dot_r.at[step, k], x_to(k)) for k in (1, 2, 3)
        ]

        for copy in big:
            copy.wait_recv()
        small = []
        for k in (1, 2, 3, 0):
            for cls in range(2):
                p, q = (x, y) if cls == 0 else (y, x)
                q = lax.rem(q + k, 4)
                value = own[cls, p, q] + big_in[step, cls, 0, q]
                value = value + (big_in[step, cls, 1, q] + big_in[step, cls, 2, q])
                mid[step, cls, q] = value
                if k:
                    small.append(
                        send(
                            mid.at[step, cls, q],
                            small_in.at[step, cls, k - 1],
                            small_s.at[step, cls, k - 1],
                            small_r.at[step, cls, k - 1],
                            (y_to if cls == 0 else x_to)(k),
                        )
                    )
        for copy in dot_copies:
            copy.wait_recv()
        dots_y[step, y] = (dots_x[step, 0] + dots_x[step, 1]) + (dots_x[step, 2] + dots_x[step, 3])
        here = dots_y.at[step, y]
        dot_copies = [
            send(here, here, dot_s.at[step, 3 + k], dot_r.at[step, 3 + k], y_to(k))
            for k in (1, 2, 3)
        ]

        for copy in small:
            copy.wait_recv()
        for cls in range(2):
            q = y if cls == 0 else x
            value = mid[step, cls, q] + small_in[step, cls, 0]
            last[step, cls] = value + (small_in[step, cls, 1] + small_in[step, cls, 2])

        def z_copy(k):
            to = lax.rem(z + k, 8)
            return pltpu.make_async_remote_copy(
                src_ref=last.at[step, to // 3, lax.rem(to, 3)],
                dst_ref=z_in.at[step, k - 1],
                send_sem=z_s.at[step, k - 1],
                recv_sem=z_r.at[step, k - 1],
                device_id=z_to(k),
                device_id_type=pl.DeviceIdType.MESH,
            )

        for k in range(1, 8):

            @pl.when(lax.rem(z + k, 8) < 6)
            def _():
                z_copy(k).start()

        for copy in dot_copies:
            copy.wait_recv()
        dots_z[step, z] = (dots_y[step, 0] + dots_y[step, 1]) + (dots_y[step, 2] + dots_y[step, 3])
        here = dots_z.at[step, z]
        dot_copies = [
            send(here, here, dot_s.at[step, 6 + k], dot_r.at[step, 6 + k], z_to(k))
            for k in range(1, 8)
        ]
        for copy in dot_copies:
            copy.wait_recv()
        pairs = [dots_z[step, 2 * i] + dots_z[step, 2 * i + 1] for i in range(4)]
        tile = (pairs[0] + pairs[1]) + (pairs[2] + pairs[3])
        rayleigh = jnp.sum(tile, axis=(0, 1), keepdims=True) * (inverse * inverse) / CELLS
        energies[step] = jnp.sum(rayleigh)

        final = step == STEPS - 1

        def zg_copy(k):
            if final:
                here = out.at[0, pl.ds(row0, 8)]
            else:
                here = fresh.at[z // 3, lax.rem(z, 3)]
            return pltpu.make_async_remote_copy(
                src_ref=here,
                dst_ref=here,
                send_sem=zg_s.at[step, k - 1],
                recv_sem=zg_r.at[step, k - 1],
                device_id=z_to(k),
                device_id_type=pl.DeviceIdType.MESH,
            )

        def zg_wait(k):
            return pltpu.make_async_remote_copy(
                src_ref=z_in.at[step, 0],
                dst_ref=z_in.at[step, 0],
                send_sem=zg_s.at[step, k - 1],
                recv_sem=zg_r.at[step, k - 1],
                device_id=z_to(k),
                device_id_type=pl.DeviceIdType.MESH,
            )

        @pl.when(z < 6)
        def _():
            for k in range(1, 8):
                pltpu.make_async_remote_copy(
                    src_ref=z_in.at[step, k - 1],
                    dst_ref=z_in.at[step, k - 1],
                    send_sem=z_s.at[step, k - 1],
                    recv_sem=z_r.at[step, k - 1],
                    device_id=z_to(k),
                    device_id_type=pl.DeviceIdType.MESH,
                ).wait_recv()
            total = last[step, z // 3, lax.rem(z, 3)]
            for k in range(7):
                total = total + z_in[step, k]
            if step == 0:
                old = psi[0, pl.ds(row0, 8)]
            else:
                old = fresh[z // 3, lax.rem(z, 3)]
            normed = old * inverse
            residual = total * inverse - rayleigh * normed
            scale = jnp.maximum(jnp.abs(diagonal[0, pl.ds(row0, 8)] - rayleigh), 1.0)
            new = normed - residual / scale
            if final:
                out[0, pl.ds(row0, 8)] = new
            else:
                fresh[z // 3, lax.rem(z, 3)] = new
            for k in range(1, 8):
                zg_copy(k).start()

        for k in range(1, 8):

            @pl.when(lax.rem(z + 8 - k, 8) < 6)
            def _():
                zg_wait(k).wait_recv()

        if not final:
            after = vecs.at[step + 1]
            grown = []
            for cls in range(2):
                p, q = (x, y) if cls == 0 else (y, x)
                after[c, cls, p, q] = fresh[cls]
                for k in (1, 2, 3):
                    grown.append(
                        send(
                            fresh.at[cls],
                            after.at[c, cls, p, q],
                            sg_s.at[cls, k - 1],
                            sg_r.at[cls, k - 1],
                            (y_to if cls == 0 else x_to)(k),
                        )
                    )
            for copy in grown:
                copy.wait_recv()
            wide = {}
            crossing = []
            for k in (1, 2, 3):
                for cls in range(2):
                    here = after.at[c, cls, x if cls == 0 else y]
                    wide[cls, k] = send(
                        here,
                        here,
                        bg_s.at[cls, k - 1],
                        bg_r.at[cls, k - 1],
                        (x_to if cls == 0 else y_to)(k),
                    )
            for k in (0, 1, 2, 3):
                for cls in range(2):
                    if k:
                        wide[cls, k].wait_recv()
                    here = after.at[c, cls, lax.rem((x if cls == 0 else y) + 4 - k, 4)]
                    crossing.append(
                        send(here, here, cg_s.at[cls, k], cg_r.at[cls, k], sibling)
                    )
            for copy in crossing:
                copy.wait_recv()
        else:
            rows = pl.ds(pl.multiple_of(96 * x + 48 * c, 8), 48)
            here = out.at[0, rows]
            wide = [None]
            crossing = []
            for k in (1, 2, 3):
                wide.append(send(here, here, bg_s.at[2, k - 1], bg_r.at[2, k - 1], x_to(k)))
            for k in (0, 1, 2, 3):
                if k:
                    wide[k].wait_recv()
                rows = pl.ds(pl.multiple_of(96 * lax.rem(x + 4 - k, 4) + 48 * c, 8), 48)
                here = out.at[0, rows]
                crossing.append(send(here, here, cg_s.at[2, k], cg_r.at[2, k], sibling))
            for copy in crossing:
                copy.wait_recv()

        for k in range(1, 8):

            @pl.when(lax.rem(z + k, 8) < 6)
            def _():
                z_copy(k).wait_send()

        @pl.when(z < 6)
        def _():
            for k in range(1, 8):
                zg_copy(k).wait_send()

    for copy in sent:
        copy.wait_send()


def shards(psi_start, diagonal, left_ops, right_ops, pair_in, pair_out, pair_count):
    vmem = pl.BlockSpec(memory_space=pltpu.VMEM)
    smem = pl.BlockSpec(memory_space=pltpu.SMEM)
    hbm = pl.BlockSpec(memory_space=pl.ANY)
    dma = pltpu.SemaphoreType.DMA
    rows = (3, 8, N)
    return pl.pallas_call(
        kernel,
        out_shape=(
            jax.ShapeDtypeStruct((1, N, N), F32),
            jax.ShapeDtypeStruct((STEPS,), F32),
        ),
        in_specs=[smem, smem, smem, vmem, vmem, hbm, hbm],
        out_specs=(vmem, smem),
        scratch_shapes=[
            pltpu.VMEM((4, N, N), F32),
            pltpu.VMEM((4, N, N), F32),
            pltpu.VMEM((4, 2, N // 2, 3 * N), BF16),
            pltpu.VMEM((4, 3 * N, N), BF16),
            pltpu.VMEM((4, N, 3 * N), BF16),
            pltpu.VMEM((4, 3 * N, N), BF16),
            pltpu.VMEM((4, N // 2, N), F32),
            pltpu.VMEM((STEPS, 2, 2, 4, 4, *rows), F32),
            pltpu.VMEM((STEPS, 2, 4, 4, *rows), F32),
            pltpu.VMEM((STEPS, 2, 4, 4, *rows), F32),
            pltpu.VMEM((STEPS, 2, 4, 4, *rows), F32),
            pltpu.VMEM((STEPS, 2, 3, 4, *rows), F32),
            pltpu.VMEM((STEPS, 2, 4, *rows), F32),
            pltpu.VMEM((STEPS, 2, 3, *rows), F32),
            pltpu.VMEM((STEPS, 2, *rows), F32),
            pltpu.VMEM((STEPS, 7, 8, N), F32),
            pltpu.VMEM((2, *rows), F32),
            pltpu.VMEM((STEPS, 2, 8, 128), F32),
            pltpu.VMEM((STEPS, 4, 8, 128), F32),
            pltpu.VMEM((STEPS, 4, 8, 128), F32),
            pltpu.VMEM((STEPS, 8, 8, 128), F32),
            dma((2,)),
            dma((5, 3)),
            dma((5, 3)),
            dma((3, 5)),
            dma((3, 5)),
            dma((STEPS,)),
            dma((STEPS,)),
            dma((STEPS, 2, 3)),
            dma((STEPS, 2, 3)),
            dma((STEPS, 2, 3)),
            dma((STEPS, 2, 3)),
            dma((STEPS, 7)),
            dma((STEPS, 7)),
            dma((STEPS, 7)),
            dma((STEPS, 7)),
            dma((2, 3)),
            dma((2, 3)),
            dma((3, 3)),
            dma((3, 3)),
            dma((3, 4)),
            dma((3, 4)),
            dma((STEPS, 14)),
            dma((STEPS, 14)),
        ],
        compiler_params=pltpu.CompilerParams(
            collective_id=0, has_side_effects=True, vmem_limit_bytes=52 * 1024 * 1024
        ),
    )(pair_in, pair_out, pair_count, psi_start, diagonal, left_ops, right_ops)


def solution(mesh):
    both = ("term", "sector")
    in_specs = (
        P("sector", None, None),
        P("sector", None, None),
        P(both, None, None),
        P(both, None, None),
        P(both, None),
        P(both, None),
        P(both),
    )
    out_specs = (P("sector", None, None), P())
    return jax.shard_map(
        shards, mesh=mesh, in_specs=in_specs, out_specs=out_specs, check_vma=False
    )
```

time: 501 us -> 115 us (0.23)
  blocking collectives: 340 us -> 0 us
  Pallas kernels: 0 us -> 109 us
  waiting for transfers between devices: 72 us -> 0 us
  matrix products: 19.3 us -> 0 us
  loops' own time: 19.2 us -> 0 us
  starting transfers between devices: 14.9 us -> 0 us
  other arithmetic: 14.5 us -> 0 us
  local copies, waits for them, and re-layouts: 16 us -> 4.76 us
    all_to_all x5 -> x0, blocking collectives: 183 us -> none  [the longest x4 157 us: sent_and_summed(): lax.all_to_all(pieces, axis, split_axis=0, concat_axis=0, tiled=True)]
    psum x16 -> x0, blocking collectives: 157 us -> none  [over_axes(): return functools.reduce(lax.psum, axes, array)]
    pallas_call x0 -> x1, Pallas kernels: none -> 109 us  [shards(): pl.pallas_call(kernel, out_shape=(jax.ShapeDtypeStruct((1, N, N), F32), j...]
    all_to_all x3 -> x0, waiting for transfers between devices: 72 us -> none  [copy_for_each(): return lax.all_to_all(copies, axis, split_axis=0, concat_axis=0, tiled=True)]
    dot_general x8 -> x0, matrix products: 19.3 us -> none  [the longest x4 10 us: one_pair(): inner_prod = jnp.dot(left_block, source, precision=lax.Precision.HIGHEST)]
    another operation x2 -> x0, loops' own time: 19.2 us -> none  [apply_pairs(): lax.fori_loop(0, pair_count[0], one_pair, jnp.zeros(gathered.shape, jnp.f...]
    all_to_all x3 -> x0, starting transfers between devices: 14.9 us -> none  [copy_for_each(): return lax.all_to_all(copies, axis, split_axis=0, concat_axis=0, tiled=True)]
    reduce_sum x8 -> x0, other arithmetic: 9.18 us -> none  [the longest x4 4.42 us: sent_and_summed(): return arrived.sum(axis=0)]
  transfers between devices with their start and end apart: 3 -> 0, of which waited for: 3 -> 0; matrix products, arithmetic and copies ran while one was open for 0% -> 0% of each run, Pallas kernels for 0% -> 0%
where the time goes in v1:
time: 115 us
  Pallas kernels  109 us (95%)
  local copies, waits for them, and re-layouts  4.76 us (4%)
  between operations  1.3 us (1%)
    pallas_call x1, Pallas kernels, shards(): pl.pallas_call(kernel, out_shape=(jax.ShapeDtypeStruct((1, N, N), F32), j...  109 us
    unnamed x10, local copies, waits for them, and re-layouts  4.76 us

profile of v1, /device:TPU:1, one launch (start us, length us, event | category | flops | bytes accessed | tf_op | source)
XLA Modules:
  0.0 114.9 jit_solution(14461563426238761349)
XLA Ops:
  1.3 0.0 copy-start
  1.3 1.1 copy-done
  2.3 0.0 copy-start.1
  2.3 1.1 copy-done.1
  3.4 0.0 copy-start.2
  3.4 0.7 copy-done.2
  4.1 0.0 copy-start.3
  4.1 0.7 copy-done.3
  4.7 108.9 %shard_map.86 = (f32[1,384,384]{2,1,0:T(8,128)S(1)}, f32[2]{0:T(128)S(1)}) custom-call(s32[1,4]{1,0:T(1,128)S(1)} %copy-done.2, s32[1,4]{1,0:T(1,128)S(1)} %copy-done.3, s32[1]{0:T(128)S(6)} %copy.11.pair_count, f32[1,384,384]{2,1,0:T(8,128)S(1)} %copy-done, f32[1,384,384]{2,1,0:T(8,128)S(1)} %copy-done.1, f32[4,384,384]{2,1,0:T(8,128)} %left_hbm.1, ...), custom_call_target="tpu_custom_call" | custom-call | tf_op jit(solution)/shard_map/pallas_call | solution.py:489
  113.6 0.8 copy.12
  114.4 0.5 copy.13
Async XLA Ops:
  1.3 1.1 copy-start
  2.3 1.1 copy-start.1
  3.4 0.7 copy-start.2
  4.1 0.7 copy-start.3

commit v2 on v0

v2 whole, which is shorter than its diff:
```python
import functools

import jax
import jax.numpy as jnp
from jax import lax
from jax.experimental import pallas as pl
from jax.experimental.pallas import tpu as pltpu
from jax.sharding import PartitionSpec as P

STEPS = 2
EPSILON = 1e-06
N = 384
CELLS = float(4 * N * N)
F32 = jnp.float32
BF16 = jnp.bfloat16


def matmul(a, b):
    return lax.dot_general(a, b, (((1,), (0,)), ((), ())), preferred_element_type=F32)


def halves(value):
    high = value.astype(BF16)
    return high, (value - high.astype(F32)).astype(BF16)


def kernel(
    pair_in_hbm,
    pair_out_hbm,
    pair_count_hbm,
    psi_hbm,
    diagonal_hbm,
    left_hbm,
    right_hbm,
    out,
    energies,
    pair_in,
    pair_out,
    pair_count,
    psi,
    diagonal,
    left,
    right,
    left3,
    right3,
    vec3,
    inner3,
    product,
    vecs,
    part_far,
    part_near,
    core_in,
    big_in,
    mid,
    small_in,
    last,
    z_in,
    fresh,
    dots_c,
    dots_z,
    dots_x,
    dots_y,
    load_sem,
    init_s,
    init_r,
    init_cs,
    init_cr,
    core_s,
    core_r,
    big_s,
    big_r,
    small_s,
    small_r,
    z_s,
    z_r,
    zg_s,
    zg_r,
    sg_s,
    sg_r,
    bg_s,
    bg_r,
    cg_s,
    cg_r,
    dot_s,
    dot_r,
):
    t = lax.axis_index("term")
    y = lax.axis_index("sector")
    z = t // 8
    x = lax.rem(t // 2, 4)
    c = lax.rem(t, 2)
    d = 1 - c

    def device(z_, x_, c_, y_):
        return ((z_ * 4 + x_) * 2 + c_, y_)

    def x_to(k):
        return device(z, lax.rem(x + k, 4), c, y)

    def y_to(k):
        return device(z, x, c, lax.rem(y + k, 4))

    def z_to(k):
        return device(lax.rem(z + k, 8), x, c, y)

    sibling = device(z, x, d, y)

    p_me, q_me = (x, y), (y, x)
    p_to, q_to = (x_to, y_to), (y_to, x_to)

    barrier = pltpu.get_barrier_semaphore()
    peers = [z_to(k) for k in (4, 3, 5, 2, 6, 1, 7)]
    peers += [x_to(k) for k in (2, 1, 3)]
    peers += [y_to(k) for k in (2, 1, 3)]
    peers += [sibling]
    for peer in peers:
        pl.semaphore_signal(barrier, inc=1, device_id=peer, device_id_type=pl.DeviceIdType.MESH)

    loads = {}
    for index, (name, source, target) in enumerate(
        (
            ("psi", psi_hbm, psi),
            ("right", right_hbm, right),
            ("left", left_hbm, left),
            ("in", pair_in_hbm, pair_in),
            ("out", pair_out_hbm, pair_out),
            ("count", pair_count_hbm, pair_count),
            ("diagonal", diagonal_hbm, diagonal),
        )
    ):
        loads[name] = pltpu.make_async_copy(source, target, load_sem.at[index])
        loads[name].start()

    sent = []

    def remote(source, target, send_sem, recv_sem, peer):
        return pltpu.make_async_remote_copy(
            src_ref=source,
            dst_ref=target,
            send_sem=send_sem,
            recv_sem=recv_sem,
            device_id=peer,
            device_id_type=pl.DeviceIdType.MESH,
        )

    def send(source, target, send_sem, recv_sem, peer):
        copy = remote(source, target, send_sem, recv_sem, peer)
        copy.start()
        sent.append(copy)
        return copy

    first = vecs.at[0]
    loads["psi"].wait()
    for cc in range(2):
        for xx in range(4):
            row = 96 * xx + 48 * cc
            first[cc, 0, y, xx] = psi[0, row : row + 24].reshape(3, 8, N)
            first[cc, 1, xx, y] = psi[0, row + 24 : row + 48].reshape(3, 8, N)

    loads["right"].wait()

    def split_right(j, carry):
        high, low = halves(right[j].T)
        right3[j, 0:N] = high
        right3[j, N : 2 * N] = high
        right3[j, 2 * N :] = low
        return carry

    lax.fori_loop(0, 4, split_right, 0)

    pl.semaphore_wait(barrier, len(peers))

    near = []
    whole = []
    for k in (1, 2, 3):
        here = first.at[c, 0, y, x]
        near.append(send(here, here, init_s.at[0, k - 1], init_r.at[0, k - 1], y_to(k)))
    for k in (1, 2, 3):
        here = first.at[c, 1, :, y]
        whole.append(send(here, here, init_s.at[1, k - 1], init_r.at[1, k - 1], y_to(k)))

    loads["left"].wait()

    def split_left(j, carry):
        for cc in range(2):
            for xx in range(4):
                row = 96 * xx + 48 * cc
                high, low = halves(left[j, row : row + 48])
                rows = slice(48 * xx, 48 * xx + 48)
                left3[j, cc, rows, 0:N] = high
                left3[j, cc, rows, N : 2 * N] = high
                left3[j, cc, rows, 2 * N :] = low
        return carry

    lax.fori_loop(0, 4, split_left, 0)

    forward = {}
    crossing = []
    for k in (1, 3, 2):
        near[k - 1].wait_recv()
        here = first.at[c, 0, lax.rem(y + 4 - k, 4), x]
        for m in (1, 2, 3):
            forward[k, m] = send(
                here, here, init_s.at[1 + k, m - 1], init_r.at[1 + k, m - 1], x_to(m)
            )
        crossing.append(send(here, here, init_cs.at[k - 1, 0], init_cr.at[k - 1, 0], sibling))
    for name in ("in", "out", "count", "diagonal"):
        loads[name].wait()
    for k in (1, 3, 2):
        for m in (1, 3, 2):
            forward[k, m].wait_recv()
            here = first.at[c, 0, lax.rem(y + 4 - k, 4), lax.rem(x + 4 - m, 4)]
            crossing.append(send(here, here, init_cs.at[k - 1, m], init_cr.at[k - 1, m], sibling))
        whole[k - 1].wait_recv()
        here = first.at[c, 1, :, lax.rem(y + 4 - k, 4)]
        crossing.append(send(here, here, init_cs.at[k - 1, 4], init_cr.at[k - 1, 4], sibling))
    for copy in crossing:
        copy.wait_recv()

    for step in range(STEPS):
        finish_step = davidson_step(
            step, c, d, x, y, z, p_me, q_me, p_to, q_to, z_to, device, sibling, remote, send,
            out, energies, pair_in, pair_out, pair_count, psi, diagonal,
            left3, right3, vec3, inner3, product, vecs, part_far, part_near, core_in, big_in, mid,
            small_in, last, z_in, fresh, dots_c, dots_z, dots_x, dots_y,
            core_s, core_r, big_s, big_r, small_s, small_r, z_s, z_r, zg_s, zg_r,
            sg_s, sg_r, bg_s, bg_r, cg_s, cg_r, dot_s, dot_r,
        )
        finish_step()

    for copy in sent:
        copy.wait_send()


def davidson_step(
    step, c, d, x, y, z, p_me, q_me, p_to, q_to, z_to, device, sibling, remote, send,
    out, energies, pair_in, pair_out, pair_count, psi, diagonal,
    left3, right3, vec3, inner3, product, vecs, part_far, part_near, core_in, big_in, mid,
    small_in, last, z_in, fresh, dots_c, dots_z, dots_x, dots_y,
    core_s, core_r, big_s, big_r, small_s, small_r, z_s, z_r, zg_s, zg_r,
    sg_s, sg_r, bg_s, bg_r, cg_s, cg_r, dot_s, dot_r,
):
    final = step == STEPS - 1
    vec = vecs.at[step]
    row0 = pl.multiple_of(96 * x + 48 * c + 8 * z, 8)

    def convert(index, total):
        yy, xx = index // 4, lax.rem(index, 4)
        for cc in range(2):
            top = vec[cc, 0, yy, xx].reshape(24, N)
            bottom = vec[cc, 1, xx, yy].reshape(24, N)
            block = jnp.concatenate([top, bottom], axis=0)
            total = total + jnp.sum((block * block).reshape(6, 8, N), axis=0)
            high, low = halves(block)
            rows = pl.ds(pl.multiple_of(96 * xx + 48 * cc, 16), 48)
            vec3[yy, rows, 0:N] = high
            vec3[yy, rows, N : 2 * N] = low
            vec3[yy, rows, 2 * N :] = high
        return total

    squares = lax.fori_loop(0, 16, convert, jnp.zeros((8, N), F32))

    for j in range(4):
        high, low = halves(matmul(vec3[pair_in[0, j]], right3[j]))
        inner3[j, 0:N] = high
        inner3[j, N : 2 * N] = low
        inner3[j, 2 * N :] = high

    count = pair_count[0]
    targets = [pair_out[0, j] for j in range(4)]

    def combine(side, cls, q, store, total):
        def one(p, total):
            xx, yy = (p, q) if cls == 0 else (q, p)
            rows = pl.ds(pl.multiple_of(48 * xx + 24 * cls, 8), 24)
            value = jnp.zeros((24, N), F32)
            for j in range(4):
                live = jnp.logical_and(targets[j] == yy, count > j)
                value = value + jnp.where(live, product[j, rows], 0.0)
            value = value.reshape(3, 8, N)
            store(p, value)
            return total + jnp.sum(value * vec[side, cls, q, p], axis=0)

        return lax.fori_loop(0, 4, one, total)

    far, own = part_far.at[step], part_near.at[step]
    dot = jnp.zeros((8, N), F32)
    for j in range(4):
        product[j] = matmul(left3[j, d], inner3[j])
    core = {}
    for k in (1, 2, 3, 0):
        for cls in range(2):
            q = lax.rem(q_me[cls] + k, 4)

            def store_far(p, value, cls=cls, q=q):
                far[cls, q, p] = value

            dot = combine(d, cls, q, store_far, dot)
            core[cls, k] = send(
                far.at[cls, q],
                core_in.at[step, cls, q],
                core_s.at[step, cls, k],
                core_r.at[step, cls, k],
                sibling,
            )
    for j in range(4):
        product[j] = matmul(left3[j, c], inner3[j])
    big = {}
    for k in (1, 2, 3, 0):
        for cls in range(2):
            q = lax.rem(q_me[cls] + k, 4)
            core[cls, k].wait_recv()

            def store_near(p, value, cls=cls, q=q):
                own[cls, q, p] = value + core_in[step, cls, q, p]

            dot = combine(c, cls, q, store_near, dot)
            for m in (2, 1, 3):
                big[cls, k, m] = send(
                    own.at[cls, q, lax.rem(p_me[cls] + m, 4)],
                    big_in.at[step, cls, k, m - 1],
                    big_s.at[step, cls, k, m - 1],
                    big_r.at[step, cls, k, m - 1],
                    p_to[cls](m),
                )

    dots_c[step, c] = dot[:, 0:128] + dot[:, 128:256] + dot[:, 256:384]
    here = dots_c.at[step, c]
    send(here, here, dot_s.at[step, 0], dot_r.at[step, 0], sibling).wait_recv()
    dots_z[step, z] = dots_c[step, 0] + dots_c[step, 1]
    here = dots_z.at[step, z]
    dots = [send(here, here, dot_s.at[step, k], dot_r.at[step, k], z_to(k)) for k in range(1, 8)]

    mean_square = jnp.sum(squares, axis=(0, 1), keepdims=True) / CELLS + EPSILON
    inverse = 1.0 / jnp.sqrt(mean_square)

    small = {}
    for k in (1, 2, 3, 0):
        for cls in range(2):
            for m in (1, 2, 3):
                big[cls, k, m].wait_recv()
            q = lax.rem(q_me[cls] + k, 4)
            value = own[cls, q, p_me[cls]] + big_in[step, cls, k, 0]
            value = value + (big_in[step, cls, k, 1] + big_in[step, cls, k, 2])
            mid[step, cls, q] = value
            if k:
                small[cls, k] = send(
                    mid.at[step, cls, q],
                    small_in.at[step, cls, k - 1],
                    small_s.at[step, cls, k - 1],
                    small_r.at[step, cls, k - 1],
                    q_to[cls](k),
                )
        if k == 2:
            for copy in dots:
                copy.wait_recv()
            pairs = [dots_z[step, 2 * i] + dots_z[step, 2 * i + 1] for i in range(4)]
            dots_x[step, x] = (pairs[0] + pairs[1]) + (pairs[2] + pairs[3])
            here = dots_x.at[step, x]
            dots = [
                send(here, here, dot_s.at[step, 7 + m], dot_r.at[step, 7 + m], p_to[0](m))
                for m in (1, 2, 3)
            ]
    for copy in dots:
        copy.wait_recv()
    dots_y[step, y] = (dots_x[step, 0] + dots_x[step, 1]) + (dots_x[step, 2] + dots_x[step, 3])
    here = dots_y.at[step, y]
    dots = [
        send(here, here, dot_s.at[step, 10 + m], dot_r.at[step, 10 + m], p_to[1](m))
        for m in (1, 2, 3)
    ]

    def to_owner(owner):
        slot = lax.rem(owner - z + 8, 8) - 1
        return remote(
            last.at[step, owner // 3, owner % 3],
            z_in.at[step, slot],
            z_s.at[step, owner],
            z_r.at[step, slot],
            device(owner, x, c, y),
        )

    for cls in range(2):
        for k in (1, 2, 3):
            small[cls, k].wait_recv()
        value = mid[step, cls, q_me[cls]] + small_in[step, cls, 0]
        last[step, cls] = value + (small_in[step, cls, 1] + small_in[step, cls, 2])
        for owner in range(3 * cls, 3 * cls + 3):

            @pl.when(z != owner)
            def _(owner=owner):
                to_owner(owner).start()

    for copy in dots:
        copy.wait_recv()
    tile = (dots_y[step, 0] + dots_y[step, 1]) + (dots_y[step, 2] + dots_y[step, 3])
    rayleigh = jnp.sum(tile, axis=(0, 1), keepdims=True) * (inverse * inverse) / CELLS

    def from_owner(owner, peer):
        if final:
            here = out.at[0, pl.ds(pl.multiple_of(96 * x + 48 * c + 8 * owner, 8), 8)]
        else:
            here = fresh.at[owner // 3, lax.rem(owner, 3)]
        return here, peer

    def spread(k):
        here, peer = from_owner(z, z_to(k))
        return remote(here, here, zg_s.at[step, k - 1], zg_r.at[step, z], peer)

    @pl.when(z < 6)
    def _():
        if step == 0:
            old = psi[0, pl.ds(row0, 8)]
        else:
            old = fresh[z // 3, lax.rem(z, 3)]
        normed = old * inverse
        scale = jnp.maximum(jnp.abs(diagonal[0, pl.ds(row0, 8)] - rayleigh), 1.0)
        total = last[step, z // 3, lax.rem(z, 3)]
        for k in range(1, 8):
            remote(
                z_in.at[step, k - 1],
                z_in.at[step, k - 1],
                z_s.at[step, 0],
                z_r.at[step, k - 1],
                z_to(k),
            ).wait_recv()
            total = total + z_in[step, k - 1]
        residual = total * inverse - rayleigh * normed
        new = normed - residual / scale
        if final:
            out[0, pl.ds(row0, 8)] = new
        else:
            fresh[z // 3, lax.rem(z, 3)] = new
        for k in (4, 3, 5, 2, 6, 1, 7):
            spread(k).start()

    energies[step] = jnp.sum(rayleigh)

    def wait_owners(cls):
        for owner in range(3 * cls, 3 * cls + 3):

            @pl.when(z != owner)
            def _(owner=owner):
                remote(
                    z_in.at[step, 0],
                    z_in.at[step, 0],
                    zg_s.at[step, 0],
                    zg_r.at[step, owner],
                    device(owner, x, c, y),
                ).wait_recv()

    wide = {}
    crossing = []
    if not final:
        after = vecs.at[step + 1]
        grown = {}
        for cls in range(2):
            wait_owners(cls)
            here, there = fresh.at[cls], after.at[c, cls, q_me[cls], p_me[cls]]
            for k in (2, 1, 3):
                grown[cls, k] = send(
                    here, there, sg_s.at[cls, k - 1], sg_r.at[cls, k - 1], q_to[cls](k)
                )
            for m in (2, 1, 3):
                wide[cls, 0, m] = send(
                    here, there, bg_s.at[cls, 0, m - 1], bg_r.at[cls, 0, m - 1], p_to[cls](m)
                )
            crossing.append(send(here, there, cg_s.at[cls, 0, 0], cg_r.at[cls, 0, 0], sibling))
            after[c, cls, q_me[cls], p_me[cls]] = fresh[cls]
        for k in (1, 3, 2):
            for cls in range(2):
                grown[cls, k].wait_recv()
                here = after.at[c, cls, lax.rem(q_me[cls] + 4 - k, 4), p_me[cls]]
                for m in (2, 1, 3):
                    wide[cls, k, m] = send(
                        here, here, bg_s.at[cls, k, m - 1], bg_r.at[cls, k, m - 1], p_to[cls](m)
                    )
                crossing.append(send(here, here, cg_s.at[cls, k, 0], cg_r.at[cls, k, 0], sibling))
        for k in (0, 1, 3, 2):
            for m in (1, 3, 2):
                for cls in range(2):
                    wide[cls, k, m].wait_recv()
                    q, p = lax.rem(q_me[cls] + 4 - k, 4), lax.rem(p_me[cls] + 4 - m, 4)
                    here = after.at[c, cls, q, p]
                    crossing.append(
                        send(here, here, cg_s.at[cls, k, m], cg_r.at[cls, k, m], sibling)
                    )
    else:

        def rows(cls, xx):
            return out.at[0, pl.ds(pl.multiple_of(96 * xx + 48 * c + 24 * cls, 8), 24)]

        for cls in range(2):
            wait_owners(cls)
            here = rows(cls, x)
            for m in (2, 1, 3):
                wide[cls, m] = send(
                    here, here, bg_s.at[cls, 4, m - 1], bg_r.at[cls, 4, m - 1], p_to[0](m)
                )
            crossing.append(send(here, here, cg_s.at[cls, 4, 0], cg_r.at[cls, 4, 0], sibling))
        for m in (1, 3, 2):
            for cls in range(2):
                wide[cls, m].wait_recv()
                here = rows(cls, lax.rem(x + 4 - m, 4))
                crossing.append(send(here, here, cg_s.at[cls, 4, m], cg_r.at[cls, 4, m], sibling))
    for copy in crossing:
        copy.wait_recv()

    def finish():
        for owner in range(6):

            @pl.when(z != owner)
            def _(owner=owner):
                to_owner(owner).wait_send()

        @pl.when(z < 6)
        def _():
            for k in range(1, 8):
                spread(k).wait_send()

    return finish


def shards(psi_start, diagonal, left_ops, right_ops, pair_in, pair_out, pair_count):
    vmem = pl.BlockSpec(memory_space=pltpu.VMEM)
    smem = pl.BlockSpec(memory_space=pltpu.SMEM)
    hbm = pl.BlockSpec(memory_space=pl.ANY)
    dma = pltpu.SemaphoreType.DMA
    rows = (3, 8, N)
    pieces = (2, 4, 4, *rows)
    return pl.pallas_call(
        kernel,
        out_shape=(
            jax.ShapeDtypeStruct((1, N, N), F32),
            jax.ShapeDtypeStruct((STEPS,), F32),
        ),
        in_specs=[hbm] * 7,
        out_specs=(vmem, smem),
        scratch_shapes=[
            pltpu.SMEM((1, 4), jnp.int32),
            pltpu.SMEM((1, 4), jnp.int32),
            pltpu.SMEM((1,), jnp.int32),
            pltpu.VMEM((1, N, N), F32),
            pltpu.VMEM((1, N, N), F32),
            pltpu.VMEM((4, N, N), F32),
            pltpu.VMEM((4, N, N), F32),
            pltpu.VMEM((4, 2, N // 2, 3 * N), BF16),
            pltpu.VMEM((4, 3 * N, N), BF16),
            pltpu.VMEM((4, N, 3 * N), BF16),
            pltpu.VMEM((4, 3 * N, N), BF16),
            pltpu.VMEM((4, N // 2, N), F32),
            pltpu.VMEM((STEPS, 2, *pieces), F32),
            pltpu.VMEM((STEPS, *pieces), F32),
            pltpu.VMEM((STEPS, *pieces), F32),
            pltpu.VMEM((STEPS, *pieces), F32),
            pltpu.VMEM((STEPS, 2, 4, 3, *rows), F32),
            pltpu.VMEM((STEPS, 2, 4, *rows), F32),
            pltpu.VMEM((STEPS, 2, 3, *rows), F32),
            pltpu.VMEM((STEPS, 2, *rows), F32),
            pltpu.VMEM((STEPS, 7, 8, N), F32),
            pltpu.VMEM((2, *rows), F32),
            pltpu.VMEM((STEPS, 2, 8, 128), F32),
            pltpu.VMEM((STEPS, 8, 8, 128), F32),
            pltpu.VMEM((STEPS, 4, 8, 128), F32),
            pltpu.VMEM((STEPS, 4, 8, 128), F32),
            dma((7,)),
            dma((5, 3)),
            dma((5, 3)),
            dma((3, 5)),
            dma((3, 5)),
            dma((STEPS, 2, 4)),
            dma((STEPS, 2, 4)),
            dma((STEPS, 2, 4, 3)),
            dma((STEPS, 2, 4, 3)),
            dma((STEPS, 2, 3)),
            dma((STEPS, 2, 3)),
            dma((STEPS, 6)),
            dma((STEPS, 7)),
            dma((STEPS, 7)),
            dma((STEPS, 6)),
            dma((2, 3)),
            dma((2, 3)),
            dma((2, 5, 3)),
            dma((2, 5, 3)),
            dma((2, 5, 4)),
            dma((2, 5, 4)),
            dma((STEPS, 14)),
            dma((STEPS, 14)),
        ],
        compiler_params=pltpu.CompilerParams(
            collective_id=0, has_side_effects=True, vmem_limit_bytes=52 * 1024 * 1024
        ),
    )(pair_in, pair_out, pair_count, psi_start, diagonal, left_ops, right_ops)


def solution(mesh):
    both = ("term", "sector")
    in_specs = (
        P("sector", None, None),
        P("sector", None, None),
        P(both, None, None),
        P(both, None, None),
        P(both, None),
        P(both, None),
        P(both),
    )
    out_specs = (P("sector", None, None), P())
    return jax.shard_map(
        shards, mesh=mesh, in_specs=in_specs, out_specs=out_specs, check_vma=False
    )
```

time: 501 us -> 105 us (0.21)
  blocking collectives: 340 us -> 0 us
  Pallas kernels: 0 us -> 98.6 us
  waiting for transfers between devices: 72 us -> 0 us
  matrix products: 19.3 us -> 0 us
  loops' own time: 19.2 us -> 0 us
  starting transfers between devices: 14.9 us -> 0 us
  other arithmetic: 14.5 us -> 0 us
  local copies, waits for them, and re-layouts: 16 us -> 4.76 us
    all_to_all x5 -> x0, blocking collectives: 183 us -> none  [the longest x4 157 us: sent_and_summed(): lax.all_to_all(pieces, axis, split_axis=0, concat_axis=0, tiled=True)]
    psum x16 -> x0, blocking collectives: 157 us -> none  [over_axes(): return functools.reduce(lax.psum, axes, array)]
    pallas_call x0 -> x1, Pallas kernels: none -> 98.6 us  [shards(): pl.pallas_call(kernel, out_shape=(jax.ShapeDtypeStruct((1, N, N), F32), j...]
    all_to_all x3 -> x0, waiting for transfers between devices: 72 us -> none  [copy_for_each(): return lax.all_to_all(copies, axis, split_axis=0, concat_axis=0, tiled=True)]
    dot_general x8 -> x0, matrix products: 19.3 us -> none  [the longest x4 10 us: one_pair(): inner_prod = jnp.dot(left_block, source, precision=lax.Precision.HIGHEST)]
    another operation x2 -> x0, loops' own time: 19.2 us -> none  [apply_pairs(): lax.fori_loop(0, pair_count[0], one_pair, jnp.zeros(gathered.shape, jnp.f...]
    all_to_all x3 -> x0, starting transfers between devices: 14.9 us -> none  [copy_for_each(): return lax.all_to_all(copies, axis, split_axis=0, concat_axis=0, tiled=True)]
    reduce_sum x8 -> x0, other arithmetic: 9.18 us -> none  [the longest x4 4.42 us: sent_and_summed(): return arrived.sum(axis=0)]
  transfers between devices with their start and end apart: 3 -> 0, of which waited for: 3 -> 0; matrix products, arithmetic and copies ran while one was open for 0% -> 0% of each run, Pallas kernels for 0% -> 0%
where the time goes in v2:
time: 105 us
  Pallas kernels  98.6 us (94%)
  local copies, waits for them, and re-layouts  4.76 us (5%)
  between operations  1.3 us (1%)
    pallas_call x1, Pallas kernels, shards(): pl.pallas_call(kernel, out_shape=(jax.ShapeDtypeStruct((1, N, N), F32), j...  98.6 us
    unnamed x10, local copies, waits for them, and re-layouts  4.76 us

profile of v2, /device:TPU:1, one launch (start us, length us, event | category | flops | bytes accessed | tf_op | source)
XLA Modules:
  0.0 104.6 jit_solution(15982470127109700258)
XLA Ops:
  1.3 0.0 copy-start
  1.3 1.1 %copy-done = f32[1,384,384]{2,1,0:T(8,128)S(1)} copy-done((f32[1,384,384]{2,1,0:T(8,128)S(1)}, f32[1,384,384]{2,1,0:T(8,128)}, u32[]{:S(2)}) %copy-start) | copy-done | bytes 589848
  2.3 0.0 copy-start.1
  2.3 1.1 %copy-done.1 = f32[1,384,384]{2,1,0:T(8,128)S(1)} copy-done((f32[1,384,384]{2,1,0:T(8,128)S(1)}, f32[1,384,384]{2,1,0:T(8,128)}, u32[]{:S(2)}) %copy-start.1) | copy-done | bytes 589848
  3.4 0.0 copy-start.2
  3.4 0.7 copy-done.2
  4.1 0.0 copy-start.3
  4.1 0.7 copy-done.3
  4.7 98.6 %shard_map.86 = (f32[1,384,384]{2,1,0:T(8,128)S(1)}, f32[2]{0:T(128)S(1)}) custom-call(s32[1,4]{1,0:T(1,128)S(1)} %copy-done.2, s32[1,4]{1,0:T(1,128)S(1)} %copy-done.3, s32[1]{0:T(128)S(6)} %copy.11.pair_count_hbm, f32[1,384,384]{2,1,0:T(8,128)S(1)} %copy-done, f32[1,384,384]{2,1,0:T(8,128)S(1)} %copy-done.1, f32[4,384,384]{2,1,0:T(8,128)} %left_hbm.1, ...), custom_call_target="tpu_custom_call" | custom-call | tf_op jit(solution)/shard_map/pallas_call | solution.py:531
  103.3 0.8 copy.12
  104.1 0.5 copy.13
Async XLA Ops:
  1.3 1.1 %copy-start = (f32[1,384,384]{2,1,0:T(8,128)S(1)}, f32[1,384,384]{2,1,0:T(8,128)}, u32[]{:S(2)}) copy-start(f32[1,384,384]{2,1,0:T(8,128)} %psi_hbm.1) | copy-start | bytes 1769476
  2.3 1.1 %copy-start.1 = (f32[1,384,384]{2,1,0:T(8,128)S(1)}, f32[1,384,384]{2,1,0:T(8,128)}, u32[]{:S(2)}) copy-start(f32[1,384,384]{2,1,0:T(8,128)} %diagonal_hbm.1) | copy-start | bytes 1769476
  3.4 0.7 copy-start.2
  4.1 0.7 copy-start.3

commit v3 on v0

v3 whole, which is shorter than its diff:
```python
import functools

import jax
import jax.numpy as jnp
from jax import lax
from jax.experimental import pallas as pl
from jax.experimental.pallas import tpu as pltpu
from jax.sharding import PartitionSpec as P

STEPS = 2
EPSILON = 1e-06
N = 384
CELLS = float(4 * N * N)
F32 = jnp.float32
BF16 = jnp.bfloat16


def matmul(a, b):
    return lax.dot_general(a, b, (((1,), (0,)), ((), ())), preferred_element_type=F32)


def halves(value):
    high = value.astype(BF16)
    return high, (value - high.astype(F32)).astype(BF16)


def kernel(
    pair_in_hbm,
    pair_out_hbm,
    pair_count_hbm,
    psi,
    diagonal,
    left_hbm,
    right_hbm,
    out,
    energies,
    pair_in,
    pair_out,
    pair_count,
    diagonal_own,
    left,
    right,
    left3,
    right3,
    vec3,
    inner3,
    product,
    vecs,
    part_far,
    part_near,
    core_in,
    big_in,
    mid,
    small_in,
    last,
    z_in,
    fresh,
    dots,
    load_sem,
    near_s,
    near_r,
    whole_s,
    whole_r,
    forward_s,
    forward_r,
    core_s,
    core_r,
    big_s,
    big_r,
    small_s,
    small_r,
    z_s,
    z_r,
    owner_s,
    owner_r,
    grow_s,
    grow_r,
    wide_s,
    wide_r,
    cross_s,
    cross_r,
    end_s,
    end_r,
    dot_s,
    dot_r,
):
    t = lax.axis_index("term")
    y = lax.axis_index("sector")
    z = t // 8
    x = lax.rem(t // 2, 4)
    c = lax.rem(t, 2)
    d = 1 - c

    def device(z_, x_, c_, y_):
        return ((z_ * 4 + x_) * 2 + c_, y_)

    def x_to(k):
        return device(z, lax.rem(x + k, 4), c, y)

    def y_to(k):
        return device(z, x, c, lax.rem(y + k, 4))

    def z_to(k):
        return device(lax.rem(z + k, 8), x, c, y)

    sibling = device(z, x, d, y)

    p_me, q_me = (x, y), (y, x)
    p_to, q_to = (x_to, y_to), (y_to, x_to)

    barrier = pltpu.get_barrier_semaphore()
    peers = [z_to(k) for k in (4, 3, 5, 2, 6, 1, 7)]
    peers += [x_to(k) for k in (2, 1, 3)]
    peers += [y_to(k) for k in (2, 1, 3)]
    peers += [sibling]
    for peer in peers:
        pl.semaphore_signal(barrier, inc=1, device_id=peer, device_id_type=pl.DeviceIdType.MESH)

    first = vecs.at[0]
    owner = jnp.minimum(z, 5)
    loads = []
    for source, target in (
        (right_hbm, right),
        (left_hbm, left),
        (psi.at[x, c, owner // 3, lax.rem(owner, 3)], fresh.at[0, owner // 3, lax.rem(owner, 3)]),
        (diagonal.at[x, c, owner // 3, lax.rem(owner, 3)], diagonal_own),
        (psi.at[:, 0, 0], first.at[0, 0, y]),
        (psi.at[:, 1, 0], first.at[1, 0, y]),
        (psi.at[:, 0, 1], first.at[0, 1, :, y]),
        (psi.at[:, 1, 1], first.at[1, 1, :, y]),
        (pair_in_hbm, pair_in),
        (pair_out_hbm, pair_out),
        (pair_count_hbm, pair_count),
    ):
        load = pltpu.make_async_copy(source, target, load_sem.at[len(loads)])
        load.start()
        loads.append(load)

    def remote(source, target, send_sem, recv_sem, peer):
        return pltpu.make_async_remote_copy(
            src_ref=source,
            dst_ref=target,
            send_sem=send_sem,
            recv_sem=recv_sem,
            device_id=peer,
            device_id_type=pl.DeviceIdType.MESH,
        )

    def send(source, target, send_sem, recv_sem, peer):
        remote(source, target, send_sem, recv_sem, peer).start()

    def arrived(like, sem):
        remote(like, like, sem, sem, sibling).wait_recv()

    def left_here(like, sem):
        remote(like, like, sem, sem, sibling).wait_send()

    pl.semaphore_wait(barrier, len(peers))

    for k in (2, 1, 3):
        send(psi.at[x, c, 0], first.at[c, 0, y, x], near_s, near_r.at[k - 1], y_to(k))
    for k in (2, 1, 3):
        send(psi.at[:, c, 1], first.at[c, 1, :, y], whole_s, whole_r.at[k - 1], y_to(k))

    loads[0].wait()

    def split_right(j, carry):
        high, low = halves(right[j].T)
        right3[j, 0:N] = high
        right3[j, N : 2 * N] = high
        right3[j, 2 * N :] = low
        return carry

    lax.fori_loop(0, 4, split_right, 0)

    def forward(k, carry):
        here = first.at[c, 0, lax.rem(y + 4 - k, 4), x]
        arrived(here, near_r.at[k - 1])
        for m in (2, 1, 3):
            send(here, here, forward_s, forward_r.at[k - 1], x_to(m))
        return carry

    lax.fori_loop(1, 4, forward, 0)

    loads[1].wait()

    def split_left(j, carry):
        for cc in range(2):
            for xx in range(4):
                row = 96 * xx + 48 * cc
                high, low = halves(left[j, row : row + 48])
                rows = slice(48 * xx, 48 * xx + 48)
                left3[j, cc, rows, 0:N] = high
                left3[j, cc, rows, N : 2 * N] = high
                left3[j, cc, rows, 2 * N :] = low
        return carry

    lax.fori_loop(0, 4, split_left, 0)

    for load in loads[2:]:
        load.wait()

    def cross(k, carry):
        sector = lax.rem(y + 4 - k, 4)
        arrived(big_in.at[0, 0, 0], forward_r.at[k - 1])
        here = first.at[c, 0, sector]
        send(here, here, cross_s.at[STEPS], cross_r.at[STEPS], sibling)
        here = first.at[c, 1, :, sector]
        arrived(here, whole_r.at[k - 1])
        send(here, here, cross_s.at[STEPS], cross_r.at[STEPS], sibling)
        return carry

    lax.fori_loop(1, 4, cross, 0)
    arrived(big_in.at[0], cross_r.at[STEPS])

    count = pair_count[0]
    targets = [pair_out[0, j] for j in range(4)]

    def davidson_step(step, carry):
        vec = vecs.at[step]

        def convert(index, total):
            yy, xx = index // 4, lax.rem(index, 4)
            for cc in range(2):
                top = vec[cc, 0, yy, xx].reshape(24, N)
                bottom = vec[cc, 1, xx, yy].reshape(24, N)
                block = jnp.concatenate([top, bottom], axis=0)
                total = total + jnp.sum((block * block).reshape(6, 8, N), axis=0)
                high, low = halves(block)
                rows = pl.ds(pl.multiple_of(96 * xx + 48 * cc, 16), 48)
                vec3[yy, rows, 0:N] = high
                vec3[yy, rows, N : 2 * N] = low
                vec3[yy, rows, 2 * N :] = high
            return total

        squares = lax.fori_loop(0, 16, convert, jnp.zeros((8, N), F32))

        for j in range(4):
            high, low = halves(matmul(vec3[pair_in[0, j]], right3[j]))
            inner3[j, 0:N] = high
            inner3[j, N : 2 * N] = low
            inner3[j, 2 * N :] = high

        def combine(side, cls, q, p):
            xx, yy = (p, q) if cls == 0 else (q, p)
            rows = pl.ds(pl.multiple_of(48 * xx + 24 * cls, 8), 24)
            terms = []
            for j in range(4):
                live = jnp.logical_and(targets[j] == yy, count > j)
                terms.append(jnp.where(live, product[j, rows], 0.0))
            value = ((terms[0] + terms[1]) + (terms[2] + terms[3])).reshape(3, 8, N)
            return value, jnp.sum(value * vec[side, cls, q, p], axis=0)

        far, own = part_far.at[step], part_near.at[step]
        for j in range(4):
            product[j] = matmul(left3[j, d], inner3[j])

        def far_rows(i, dot):
            k = lax.rem(i + 1, 4)
            for cls in range(2):
                q = lax.rem(q_me[cls] + k, 4)
                for p in range(4):
                    value, term = combine(d, cls, q, p)
                    far[cls, q, p] = value
                    dot = dot + term
                send(
                    far.at[cls, q],
                    core_in.at[step, cls, q],
                    core_s.at[step],
                    core_r.at[step, cls, k],
                    sibling,
                )
            return dot

        dot = lax.fori_loop(0, 4, far_rows, jnp.zeros((8, N), F32))
        for j in range(4):
            product[j] = matmul(left3[j, c], inner3[j])

        def near_rows(i, dot):
            k = lax.rem(i + 1, 4)
            for cls in range(2):
                q = lax.rem(q_me[cls] + k, 4)
                arrived(core_in.at[step, cls, q], core_r.at[step, cls, k])
                for p in range(4):
                    value, term = combine(c, cls, q, p)
                    own[cls, q, p] = value + core_in[step, cls, q, p]
                    dot = dot + term
                for m in (2, 1, 3):
                    send(
                        own.at[cls, q, lax.rem(p_me[cls] + m, 4)],
                        big_in.at[step, cls, k, m - 1],
                        big_s.at[step],
                        big_r.at[step, cls, k],
                        p_to[cls](m),
                    )
            return dot

        dot = lax.fori_loop(0, 4, near_rows, dot)

        tiles = dots.at[step]
        tiles[c] = dot[:, 0:128] + dot[:, 128:256] + dot[:, 256:384]
        send(tiles.at[c], tiles.at[c], dot_s.at[step], dot_r.at[step, 0], sibling)
        arrived(tiles.at[0], dot_r.at[step, 0])
        tiles[2 + z] = tiles[0] + tiles[1]
        for k in (4, 3, 5, 2, 6, 1, 7):
            send(tiles.at[2 + z], tiles.at[2 + z], dot_s.at[step], dot_r.at[step, 1], z_to(k))

        mean_square = jnp.sum(squares, axis=(0, 1), keepdims=True) / CELLS + EPSILON
        inverse = 1.0 / jnp.sqrt(mean_square)

        def gathered(k):
            for cls in range(2):
                arrived(big_in.at[step, cls, k], big_r.at[step, cls, k])
                q = lax.rem(q_me[cls] + k, 4)
                value = own[cls, q, p_me[cls]] + big_in[step, cls, k, 0]
                mid[step, cls, q] = value + (big_in[step, cls, k, 1] + big_in[step, cls, k, 2])

        def small(k, carry):
            gathered(k)
            for cls in range(2):
                send(
                    mid.at[step, cls, lax.rem(q_me[cls] + k, 4)],
                    small_in.at[step, cls, k - 1],
                    small_s.at[step],
                    small_r.at[step, cls],
                    q_to[cls](k),
                )
            return carry

        lax.fori_loop(1, 4, small, 0)
        arrived(tiles.at[pl.ds(2, 7)], dot_r.at[step, 1])
        pairs = [tiles[2 + 2 * i] + tiles[3 + 2 * i] for i in range(4)]
        tiles[10 + x] = (pairs[0] + pairs[1]) + (pairs[2] + pairs[3])
        for k in (2, 1, 3):
            send(tiles.at[10 + x], tiles.at[10 + x], dot_s.at[step], dot_r.at[step, 2], x_to(k))
        gathered(0)
        arrived(tiles.at[pl.ds(10, 3)], dot_r.at[step, 2])
        tiles[14 + y] = (tiles[10] + tiles[11]) + (tiles[12] + tiles[13])
        for k in (2, 1, 3):
            send(tiles.at[14 + y], tiles.at[14 + y], dot_s.at[step], dot_r.at[step, 3], y_to(k))

        for cls in range(2):
            arrived(small_in.at[step, cls], small_r.at[step, cls])
            value = mid[step, cls, q_me[cls]] + small_in[step, cls, 0]
            last[step, cls] = value + (small_in[step, cls, 1] + small_in[step, cls, 2])
            for i in range(3):
                to = 3 * cls + i

                @pl.when(z != to)
                def _(to=to, cls=cls, i=i):
                    slot = lax.rem(to - z + 8, 8) - 1
                    send(
                        last.at[step, cls, i],
                        z_in.at[step, slot],
                        z_s.at[step],
                        z_r.at[step],
                        device(to, x, c, y),
                    )

        arrived(tiles.at[pl.ds(14, 3)], dot_r.at[step, 3])
        tile = (tiles[14] + tiles[15]) + (tiles[16] + tiles[17])
        rayleigh = jnp.sum(tile, axis=(0, 1), keepdims=True) * (inverse * inverse) / CELLS

        @pl.when(z < 6)
        def _():
            high, low = z // 3, lax.rem(z, 3)
            normed = fresh[step, high, low] * inverse
            scale = 1.0 / jnp.maximum(jnp.abs(diagonal_own[...] - rayleigh), 1.0)
            arrived(z_in.at[step], z_r.at[step])
            total = last[step, high, low] + z_in[step, 6]
            for i in (0, 2, 4):
                total = total + (z_in[step, i] + z_in[step, i + 1])
            residual = total * inverse - rayleigh * normed
            fresh[step + 1, high, low] = normed - residual * scale
            here = fresh.at[step + 1, high, low]
            for k in (4, 3, 5, 2, 6, 1, 7):
                send(here, here, owner_s.at[step], owner_r.at[step], z_to(k))
            arrived(z_in.at[step, pl.ds(0, 5)], owner_r.at[step])

        @pl.when(z >= 6)
        def _():
            arrived(z_in.at[step, pl.ds(0, 6)], owner_r.at[step])

        energies[step] = jnp.sum(rayleigh)

        @pl.when(step < STEPS - 1)
        def _():
            after = vecs.at[step + 1]
            for cls in range(2):
                here = fresh.at[step + 1, cls]
                there = after.at[c, cls, q_me[cls], p_me[cls]]
                for k in (2, 1, 3):
                    send(here, there, grow_s, grow_r.at[cls, k - 1], q_to[cls](k))
                for m in (2, 1, 3):
                    send(here, there, wide_s, wide_r.at[cls, 0], p_to[cls](m))
                after[c, cls, q_me[cls], p_me[cls]] = fresh[step + 1, cls]

            def grow(k, carry):
                for cls in range(2):
                    here = after.at[c, cls, lax.rem(q_me[cls] + 4 - k, 4), p_me[cls]]
                    arrived(here, grow_r.at[cls, k - 1])
                    for m in (2, 1, 3):
                        send(here, here, wide_s, wide_r.at[cls, k], p_to[cls](m))
                return carry

            lax.fori_loop(1, 4, grow, 0)

            def over(k, carry):
                for cls in range(2):
                    arrived(big_in.at[0, 0, 0], wide_r.at[cls, k])
                    here = after.at[c, cls, lax.rem(q_me[cls] + 4 - k, 4)]
                    send(here, here, cross_s.at[step], cross_r.at[step], sibling)
                return carry

            lax.fori_loop(0, 4, over, 0)
            arrived(after.at[d], cross_r.at[step])
            left_here(small_in.at[0], grow_s)
            left_here(big_in.at[0], wide_s)
            left_here(after.at[d], cross_s.at[step])

        @pl.when(step == STEPS - 1)
        def _():
            here = fresh.at[step + 1]
            for m in (2, 1, 3):
                send(here, out.at[x, c], end_s, end_r.at[m - 1], x_to(m))
            send(here, out.at[x, c], cross_s.at[step], cross_r.at[step], sibling)
            out[x, c] = fresh[step + 1]

            def over(m, carry):
                here = out.at[lax.rem(x + 4 - m, 4), c]
                arrived(here, end_r.at[m - 1])
                send(here, here, cross_s.at[step], cross_r.at[step], sibling)
                return carry

            lax.fori_loop(1, 4, over, 0)
            arrived(out.at[:, d], cross_r.at[step])
            left_here(small_in.at[0], end_s)
            left_here(out.at[:, d], cross_s.at[step])

        left_here(part_far.at[0], core_s.at[step])
        left_here(big_in.at[0], big_s.at[step])
        left_here(small_in.at[0], small_s.at[step])
        left_here(tiles.at[pl.ds(0, 14)], dot_s.at[step])

        @pl.when(z < 6)
        def _():
            left_here(z_in.at[step, pl.ds(0, 5)], z_s.at[step])
            left_here(z_in.at[step], owner_s.at[step])

        @pl.when(z >= 6)
        def _():
            left_here(z_in.at[step, pl.ds(0, 6)], z_s.at[step])

        return carry

    lax.fori_loop(0, STEPS, davidson_step, 0)

    left_here(big_in.at[0, 0, 0], near_s)
    left_here(part_far.at[0, 0, pl.ds(0, 3)], whole_s)
    left_here(big_in.at[0, 0, pl.ds(0, 3)], forward_s)
    left_here(big_in.at[0], cross_s.at[STEPS])


def shards(psi_start, diagonal, left_ops, right_ops, pair_in, pair_out, pair_count):
    vmem = pl.BlockSpec(memory_space=pltpu.VMEM)
    smem = pl.BlockSpec(memory_space=pltpu.SMEM)
    hbm = pl.BlockSpec(memory_space=pltpu.HBM)
    dma = pltpu.SemaphoreType.DMA
    rows = (3, 8, N)
    blocks = (4, 2, 2, *rows)
    pieces = (2, 4, 4, *rows)
    psi, energies = pl.pallas_call(
        kernel,
        out_shape=(
            jax.ShapeDtypeStruct(blocks, F32),
            jax.ShapeDtypeStruct((STEPS,), F32),
        ),
        in_specs=[hbm] * 7,
        out_specs=(vmem, smem),
        scratch_shapes=[
            pltpu.SMEM((1, 4), jnp.int32),
            pltpu.SMEM((1, 4), jnp.int32),
            pltpu.SMEM((1,), jnp.int32),
            pltpu.VMEM((8, N), F32),
            pltpu.VMEM((4, N, N), F32),
            pltpu.VMEM((4, N, N), F32),
            pltpu.VMEM((4, 2, N // 2, 3 * N), BF16),
            pltpu.VMEM((4, 3 * N, N), BF16),
            pltpu.VMEM((4, N, 3 * N), BF16),
            pltpu.VMEM((4, 3 * N, N), BF16),
            pltpu.VMEM((4, N // 2, N), F32),
            pltpu.VMEM((STEPS, 2, *pieces), F32),
            pltpu.VMEM((STEPS, *pieces), F32),
            pltpu.VMEM((STEPS, *pieces), F32),
            pltpu.VMEM((STEPS, *pieces), F32),
            pltpu.VMEM((STEPS, 2, 4, 3, *rows), F32),
            pltpu.VMEM((STEPS, 2, 4, *rows), F32),
            pltpu.VMEM((STEPS, 2, 3, *rows), F32),
            pltpu.VMEM((STEPS, 2, *rows), F32),
            pltpu.VMEM((STEPS, 7, 8, N), F32),
            pltpu.VMEM((STEPS + 1, 2, *rows), F32),
            pltpu.VMEM((STEPS, 18, 8, 128), F32),
            dma((11,)),
            dma,
            dma((3,)),
            dma,
            dma((3,)),
            dma,
            dma((3,)),
            dma((STEPS,)),
            dma((STEPS, 2, 4)),
            dma((STEPS,)),
            dma((STEPS, 2, 4)),
            dma((STEPS,)),
            dma((STEPS, 2)),
            dma((STEPS,)),
            dma((STEPS,)),
            dma((STEPS,)),
            dma((STEPS,)),
            dma,
            dma((2, 3)),
            dma,
            dma((2, 4)),
            dma((STEPS + 1,)),
            dma((STEPS + 1,)),
            dma,
            dma((3,)),
            dma((STEPS,)),
            dma((STEPS, 4)),
        ],
        compiler_params=pltpu.CompilerParams(
            collective_id=0, has_side_effects=True, vmem_limit_bytes=60 * 1024 * 1024
        ),
    )(
        pair_in,
        pair_out,
        pair_count,
        psi_start.reshape(blocks),
        diagonal.reshape(blocks),
        left_ops,
        right_ops,
    )
    return psi.reshape(1, N, N), energies


def solution(mesh):
    both = ("term", "sector")
    in_specs = (
        P("sector", None, None),
        P("sector", None, None),
        P(both, None, None),
        P(both, None, None),
        P(both, None),
        P(both, None),
        P(both),
    )
    out_specs = (P("sector", None, None), P())
    return jax.shard_map(
        shards, mesh=mesh, in_specs=in_specs, out_specs=out_specs, check_vma=False
    )
```

time: 501 us -> 105 us (0.21)
  blocking collectives: 340 us -> 0 us
  Pallas kernels: 0 us -> 100 us
  waiting for transfers between devices: 72 us -> 0 us
  matrix products: 19.3 us -> 0 us
  loops' own time: 19.2 us -> 0 us
  starting transfers between devices: 14.9 us -> 0 us
  other arithmetic: 14.5 us -> 0 us
  local copies, waits for them, and re-layouts: 16 us -> 3.09 us
    all_to_all x5 -> x0, blocking collectives: 183 us -> none  [the longest x4 157 us: sent_and_summed(): lax.all_to_all(pieces, axis, split_axis=0, concat_axis=0, tiled=True)]
    psum x16 -> x0, blocking collectives: 157 us -> none  [over_axes(): return functools.reduce(lax.psum, axes, array)]
    pallas_call x0 -> x1, Pallas kernels: none -> 100 us  [shards(): pl.pallas_call(kernel, out_shape=(jax.ShapeDtypeStruct(blocks, F32), jax....]
    all_to_all x3 -> x0, waiting for transfers between devices: 72 us -> none  [copy_for_each(): return lax.all_to_all(copies, axis, split_axis=0, concat_axis=0, tiled=True)]
    dot_general x8 -> x0, matrix products: 19.3 us -> none  [the longest x4 10 us: one_pair(): inner_prod = jnp.dot(left_block, source, precision=lax.Precision.HIGHEST)]
    another operation x2 -> x0, loops' own time: 19.2 us -> none  [apply_pairs(): lax.fori_loop(0, pair_count[0], one_pair, jnp.zeros(gathered.shape, jnp.f...]
    all_to_all x3 -> x0, starting transfers between devices: 14.9 us -> none  [copy_for_each(): return lax.all_to_all(copies, axis, split_axis=0, concat_axis=0, tiled=True)]
    reduce_sum x8 -> x0, other arithmetic: 9.18 us -> none  [the longest x4 4.42 us: sent_and_summed(): return arrived.sum(axis=0)]
  transfers between devices with their start and end apart: 3 -> 0, of which waited for: 3 -> 0; matrix products, arithmetic and copies ran while one was open for 0% -> 0% of each run, Pallas kernels for 0% -> 0%
where the time goes in v3:
time: 105 us; the launch traced here: 104 us
  Pallas kernels  100 us (95%)
  local copies, waits for them, and re-layouts  3.09 us (3%)
  between operations  1.29 us (1%)
    pallas_call x1, Pallas kernels, shards(): pl.pallas_call(kernel, out_shape=(jax.ShapeDtypeStruct(blocks, F32), jax....  100 us
    unnamed x2, local copies, waits for them, and re-layouts  3.09 us

profile of v3, /device:TPU:1, one launch (start us, length us, event | category | flops | bytes accessed | tf_op | source)
XLA Modules:
  0.0 104.5 jit_solution(8715139937772328883)
XLA Ops:
  1.3 100.1 %shard_map.86 = (f32[4,2,2,3,8,384]{5,4,3,2,1,0:T(8,128)}, f32[2]{0:T(128)}) custom-call(s32[1,4]{1,0:T(1,128)} %pair_in_hbm.1, s32[1,4]{1,0:T(1,128)} %pair_out_hbm.1, s32[1]{0:T(128)S(6)} %copy.11.pair_count_hbm, f32[4,2,2,3,8,384]{5,4,3,2,1,0:T(8,128)} %bitcast.3, f32[4,2,2,3,8,384]{5,4,3,2,1,0:T(8,128)} %bitcast.4, f32[4,384,384]{2,1,0:T(8,128)} %left_hbm.1, ...), custom_call_target="tpu_custom_call" | custom-call | tf_op jit(solution)/shard_map/pallas_call | solution.py:472
  101.4 1.9 %copy.12 = f32[1,384,384]{2,1,0:T(8,128)} copy(f32[1,384,384]{2,1,0:T(8,128)} %bitcast.5) | data formatting | bytes 1179648
  103.3 1.2 %copy.13 = f32[2]{0:T(128)} copy(f32[2]{0:T(128)} %get-tuple-element.9) | data formatting | bytes 16

commit v4 on v3

v4 whole, which is shorter than its diff:
```python
import functools

import jax
import jax.numpy as jnp
from jax import lax
from jax.experimental import pallas as pl
from jax.experimental.pallas import tpu as pltpu
from jax.sharding import PartitionSpec as P

STEPS = 2
EPSILON = 1e-06
N = 384
CELLS = float(4 * N * N)
F32 = jnp.float32
BF16 = jnp.bfloat16


def matmul(a, b):
    return lax.dot_general(a, b, (((1,), (0,)), ((), ())), preferred_element_type=F32)


def halves(value):
    high = value.astype(BF16)
    return high, (value - high.astype(F32)).astype(BF16)


def kernel(
    pair_in_hbm,
    pair_out_hbm,
    pair_count_hbm,
    psi,
    diagonal,
    left_hbm,
    right_hbm,
    out,
    energies,
    pair_in,
    pair_out,
    pair_count,
    diagonal_own,
    left,
    right,
    left3,
    right3,
    vec3,
    inner3,
    product,
    vecs,
    part_far,
    part_near,
    core_in,
    big_in,
    mid,
    small_in,
    last,
    z_in,
    fresh,
    dots,
    load_sem,
    near_s,
    near_r,
    whole_s,
    whole_r,
    forward_s,
    forward_r,
    core_s,
    core_r,
    big_s,
    big_r,
    small_s,
    small_r,
    z_s,
    z_r,
    owner_s,
    owner_r,
    grow_s,
    grow_r,
    wide_s,
    wide_r,
    cross_s,
    cross_r,
    end_s,
    end_r,
    dot_s,
    dot_r,
):
    t = lax.axis_index("term")
    y = lax.axis_index("sector")
    z = t // 8
    x = lax.rem(t // 2, 4)
    c = lax.rem(t, 2)
    d = 1 - c

    def device(z_, x_, c_, y_):
        return ((z_ * 4 + x_) * 2 + c_, y_)

    def x_to(k):
        return device(z, lax.rem(x + k, 4), c, y)

    def y_to(k):
        return device(z, x, c, lax.rem(y + k, 4))

    def z_to(k):
        return device(lax.rem(z + k, 8), x, c, y)

    sibling = device(z, x, d, y)

    p_me, q_me = (x, y), (y, x)
    p_to, q_to = (x_to, y_to), (y_to, x_to)

    barrier = pltpu.get_barrier_semaphore()
    peers = [z_to(k) for k in (4, 3, 5, 2, 6, 1, 7)]
    peers += [x_to(k) for k in (2, 1, 3)]
    peers += [y_to(k) for k in (2, 1, 3)]
    peers += [sibling]
    for peer in peers:
        pl.semaphore_signal(barrier, inc=1, device_id=peer, device_id_type=pl.DeviceIdType.MESH)

    first = vecs.at[0]
    owner = jnp.minimum(z, 5)
    copies = [
        (right_hbm, right),
        (left_hbm, left),
        (psi.at[x, c, owner // 3, lax.rem(owner, 3)], fresh.at[0, owner // 3, lax.rem(owner, 3)]),
        (diagonal.at[x, c, owner // 3, lax.rem(owner, 3)], diagonal_own),
        (pair_in_hbm, pair_in),
        (pair_out_hbm, pair_out),
        (pair_count_hbm, pair_count),
    ]
    for cc in range(2):
        for b in range(3):
            copies.append((psi.at[:, cc, 0, b], first.at[cc, 0, b, :, y]))
            copies.append((psi.at[:, cc, 1, b], first.at[cc, 1, b, y]))
    loads = []
    for source, target in copies:
        load = pltpu.make_async_copy(source, target, load_sem.at[len(loads)])
        load.start()
        loads.append(load)

    def remote(source, target, send_sem, recv_sem, peer):
        return pltpu.make_async_remote_copy(
            src_ref=source,
            dst_ref=target,
            send_sem=send_sem,
            recv_sem=recv_sem,
            device_id=peer,
            device_id_type=pl.DeviceIdType.MESH,
        )

    def send(source, target, send_sem, recv_sem, peer):
        remote(source, target, send_sem, recv_sem, peer).start()

    def arrived(like, sem):
        remote(like, like, sem, sem, sibling).wait_recv()

    def left_here(like, sem):
        remote(like, like, sem, sem, sibling).wait_send()

    pl.semaphore_wait(barrier, len(peers))

    for k in (2, 1, 3):
        send(psi.at[x, c, 0], first.at[c, 0, :, x, y], near_s, near_r.at[k - 1], y_to(k))
    for b in range(3):
        for k in (2, 1, 3):
            send(psi.at[:, c, 1, b], first.at[c, 1, b, y], whole_s, whole_r.at[k - 1], y_to(k))

    loads[0].wait()

    def split_right(j, carry):
        high, low = halves(right[j].T)
        right3[j, 0:N] = high
        right3[j, N : 2 * N] = high
        right3[j, 2 * N :] = low
        return carry

    lax.fori_loop(0, 4, split_right, 0)

    def forward(k, carry):
        here = first.at[c, 0, :, x, lax.rem(y + 4 - k, 4)]
        arrived(here, near_r.at[k - 1])
        for m in (2, 1, 3):
            send(here, here, forward_s, forward_r.at[k - 1], x_to(m))
        return carry

    lax.fori_loop(1, 4, forward, 0)

    loads[1].wait()

    def split_left(j, carry):
        for cc in range(2):
            for xx in range(4):
                row = 96 * xx + 48 * cc
                high, low = halves(left[j, row : row + 48])
                rows = slice(48 * xx, 48 * xx + 48)
                left3[j, cc, rows, 0:N] = high
                left3[j, cc, rows, N : 2 * N] = high
                left3[j, cc, rows, 2 * N :] = low
        return carry

    lax.fori_loop(0, 4, split_left, 0)

    for load in loads[2:]:
        load.wait()

    def cross(k, carry):
        sector = lax.rem(y + 4 - k, 4)
        arrived(small_in.at[0, 0], forward_r.at[k - 1])
        here = first.at[c, 0, :, :, sector]
        send(here, here, cross_s.at[STEPS], cross_r.at[STEPS], sibling)
        arrived(big_in.at[0, 0, 0], whole_r.at[k - 1])
        here = first.at[c, 1, :, sector]
        send(here, here, cross_s.at[STEPS], cross_r.at[STEPS], sibling)
        return carry

    lax.fori_loop(1, 4, cross, 0)
    arrived(big_in.at[0], cross_r.at[STEPS])

    count = pair_count[0]
    live = [
        [jnp.logical_and(pair_out[0, j] == yy, count > j) for yy in range(4)] for j in range(4)
    ]

    def davidson_step(step, carry):
        vec = vecs.at[step]

        def convert(index, total):
            yy, xx = index // 4, lax.rem(index, 4)
            for cc in range(2):
                top = vec[cc, 0, :, xx, yy].reshape(24, N)
                bottom = vec[cc, 1, :, yy, xx].reshape(24, N)
                block = jnp.concatenate([top, bottom], axis=0)
                total = total + jnp.sum((block * block).reshape(6, 8, N), axis=0)
                high, low = halves(block)
                rows = pl.ds(pl.multiple_of(96 * xx + 48 * cc, 16), 48)
                vec3[yy, rows, 0:N] = high
                vec3[yy, rows, N : 2 * N] = low
                vec3[yy, rows, 2 * N :] = high
            return total

        squares = lax.fori_loop(0, 16, convert, jnp.zeros((8, N), F32))

        for j in range(4):
            high, low = halves(matmul(vec3[pair_in[0, j]], right3[j]))
            inner3[j, 0:N] = high
            inner3[j, N : 2 * N] = low
            inner3[j, 2 * N :] = high

        def combine(side, cls, b, store, dot):
            for xx in range(4):
                rows = pl.ds(pl.multiple_of(48 * xx + 24 * cls + 8 * b, 8), 8)
                blocks = [product[j, rows] for j in range(4)]
                for yy in range(4):
                    p, q = (xx, yy) if cls == 0 else (yy, xx)
                    terms = [jnp.where(live[j][yy], blocks[j], 0.0) for j in range(4)]
                    value = (terms[0] + terms[1]) + (terms[2] + terms[3])
                    store(p, q, value)
                    dot = dot + value * vec[side, cls, b, p, q]
            return dot

        far, own = part_far.at[step], part_near.at[step]
        for j in range(4):
            product[j] = matmul(left3[j, d], inner3[j])

        def far_rows(b, dot):
            for cls in range(2):

                def store(p, q, value, cls=cls):
                    far[cls, b, p, q] = value

                dot = combine(d, cls, b, store, dot)
                send(
                    far.at[cls, b],
                    core_in.at[step, cls, b],
                    core_s.at[step],
                    core_r.at[step, cls, b],
                    sibling,
                )
            return dot

        dot = lax.fori_loop(0, 3, far_rows, jnp.zeros((8, N), F32))
        for j in range(4):
            product[j] = matmul(left3[j, c], inner3[j])

        def near_rows(b, dot):
            for cls in range(2):
                arrived(core_in.at[step, cls, b], core_r.at[step, cls, b])

                def store(p, q, value, cls=cls):
                    own[cls, b, p, q] = value + core_in[step, cls, b, p, q]

                dot = combine(c, cls, b, store, dot)
                for m in (2, 1, 3):
                    send(
                        own.at[cls, b, lax.rem(p_me[cls] + m, 4)],
                        big_in.at[step, cls, b, m - 1],
                        big_s.at[step],
                        big_r.at[step, cls, b],
                        p_to[cls](m),
                    )
            return dot

        dot = lax.fori_loop(0, 3, near_rows, dot)

        tiles = dots.at[step]
        tiles[c] = dot[:, 0:128] + dot[:, 128:256] + dot[:, 256:384]
        send(tiles.at[c], tiles.at[c], dot_s.at[step], dot_r.at[step, 0], sibling)
        arrived(tiles.at[0], dot_r.at[step, 0])
        tiles[2 + z] = tiles[0] + tiles[1]
        for k in (4, 3, 5, 2, 6, 1, 7):
            send(tiles.at[2 + z], tiles.at[2 + z], dot_s.at[step], dot_r.at[step, 1], z_to(k))

        mean_square = jnp.sum(squares, axis=(0, 1), keepdims=True) / CELLS + EPSILON
        inverse = 1.0 / jnp.sqrt(mean_square)

        def small(b):
            for cls in range(2):
                arrived(big_in.at[step, cls, b], big_r.at[step, cls, b])
                value = own[cls, b, p_me[cls]] + big_in[step, cls, b, 0]
                value = value + (big_in[step, cls, b, 1] + big_in[step, cls, b, 2])
                mid[step, cls, b] = value
                for k in (2, 1, 3):
                    send(
                        mid.at[step, cls, b, lax.rem(q_me[cls] + k, 4)],
                        small_in.at[step, cls, b, k - 1],
                        small_s.at[step],
                        small_r.at[step, cls, b],
                        q_to[cls](k),
                    )

        def to_owner(b):
            for cls in range(2):
                arrived(small_in.at[step, cls, b], small_r.at[step, cls, b])
                value = mid[step, cls, b, q_me[cls]] + small_in[step, cls, b, 0]
                last[step, cls, b] = value + (small_in[step, cls, b, 1] + small_in[step, cls, b, 2])
                to = 3 * cls + b

                @pl.when(z != to)
                def _(to=to, cls=cls):
                    send(
                        last.at[step, cls, b],
                        z_in.at[step, lax.rem(to - z + 8, 8) - 1],
                        z_s.at[step],
                        z_r.at[step],
                        device(to, x, c, y),
                    )

        def update(b, rayleigh):
            @pl.when(jnp.logical_or(z == b, z == b + 3))
            def _():
                high = z // 3
                normed = fresh[step, high, b] * inverse
                scale = 1.0 / jnp.maximum(jnp.abs(diagonal_own[...] - rayleigh), 1.0)
                arrived(z_in.at[step], z_r.at[step])
                total = last[step, high, b] + z_in[step, 6]
                for i in (0, 2, 4):
                    total = total + (z_in[step, i] + z_in[step, i + 1])
                residual = total * inverse - rayleigh * normed
                fresh[step + 1, high, b] = normed - residual * scale
                here = fresh.at[step + 1, high, b]
                for k in (4, 3, 5, 2, 6, 1, 7):
                    send(here, here, owner_s.at[step], owner_r.at[step, b], z_to(k))

        def from_owners(b):
            mine = jnp.logical_or(z == b, z == b + 3)

            @pl.when(mine)
            def _():
                arrived(z_in.at[step, pl.ds(0, 1)], owner_r.at[step, b])

            @pl.when(jnp.logical_not(mine))
            def _():
                arrived(z_in.at[step, pl.ds(0, 2)], owner_r.at[step, b])

        small(0)
        arrived(tiles.at[pl.ds(2, 7)], dot_r.at[step, 1])
        pairs = [tiles[2 + 2 * i] + tiles[3 + 2 * i] for i in range(4)]
        tiles[10 + x] = (pairs[0] + pairs[1]) + (pairs[2] + pairs[3])
        for k in (2, 1, 3):
            send(tiles.at[10 + x], tiles.at[10 + x], dot_s.at[step], dot_r.at[step, 2], x_to(k))
        small(1)
        to_owner(0)
        arrived(tiles.at[pl.ds(10, 3)], dot_r.at[step, 2])
        tiles[14 + y] = (tiles[10] + tiles[11]) + (tiles[12] + tiles[13])
        for k in (2, 1, 3):
            send(tiles.at[14 + y], tiles.at[14 + y], dot_s.at[step], dot_r.at[step, 3], y_to(k))
        small(2)
        to_owner(1)
        arrived(tiles.at[pl.ds(14, 3)], dot_r.at[step, 3])
        tile = (tiles[14] + tiles[15]) + (tiles[16] + tiles[17])
        rayleigh = jnp.sum(tile, axis=(0, 1), keepdims=True) * (inverse * inverse) / CELLS
        update(0, rayleigh)
        to_owner(2)
        energies[step] = jnp.sum(rayleigh)
        update(1, rayleigh)

        @pl.when(step < STEPS - 1)
        def _():
            after = vecs.at[step + 1]

            def grow(b):
                from_owners(b)
                for cls in range(2):
                    here = fresh.at[step + 1, cls, b]
                    there = after.at[c, cls, b, p_me[cls], q_me[cls]]
                    for k in (2, 1, 3):
                        send(here, there, grow_s, grow_r.at[cls, b], q_to[cls](k))
                    after[c, cls, b, p_me[cls], q_me[cls]] = fresh[step + 1, cls, b]

            def wide(b):
                for cls in range(2):
                    arrived(small_in.at[0, 0, 0], grow_r.at[cls, b])
                    here = after.at[c, cls, b, p_me[cls]]
                    for m in (2, 1, 3):
                        send(here, here, wide_s, wide_r.at[cls, b], p_to[cls](m))

            def over(b):
                for cls in range(2):
                    arrived(big_in.at[0, 0, 0], wide_r.at[cls, b])
                    here = after.at[c, cls, b]
                    send(here, here, cross_s.at[step], cross_r.at[step], sibling)

            grow(0)
            update(2, rayleigh)
            wide(0)
            grow(1)
            grow(2)
            wide(1)
            over(0)
            wide(2)
            over(1)
            over(2)
            arrived(after.at[d], cross_r.at[step])
            left_here(small_in.at[0], grow_s)
            left_here(big_in.at[0], wide_s)
            left_here(after.at[d], cross_s.at[step])

        @pl.when(step == STEPS - 1)
        def _():
            def grow(b):
                from_owners(b)
                here, there = fresh.at[step + 1, :, b], out.at[x, c, :, b]
                for m in (2, 1, 3):
                    send(here, there, end_s, end_r.at[b], x_to(m))
                out[x, c, :, b] = fresh[step + 1, :, b]

            def over(b):
                arrived(small_in.at[0, 0, pl.ds(0, 2)], end_r.at[b])
                here = out.at[:, c, :, b]
                send(here, here, cross_s.at[step], cross_r.at[step], sibling)

            grow(0)
            update(2, rayleigh)
            grow(1)
            over(0)
            grow(2)
            over(1)
            over(2)
            arrived(out.at[:, d], cross_r.at[step])
            left_here(small_in.at[0], end_s)
            left_here(out.at[:, d], cross_s.at[step])

        left_here(part_far.at[0], core_s.at[step])
        left_here(big_in.at[0], big_s.at[step])
        left_here(small_in.at[0], small_s.at[step])
        left_here(tiles.at[pl.ds(0, 14)], dot_s.at[step])

        @pl.when(z < 6)
        def _():
            left_here(z_in.at[step, pl.ds(0, 5)], z_s.at[step])
            left_here(z_in.at[step], owner_s.at[step])

        @pl.when(z >= 6)
        def _():
            left_here(z_in.at[step, pl.ds(0, 6)], z_s.at[step])

        return carry

    lax.fori_loop(0, STEPS, davidson_step, 0)

    left_here(small_in.at[0, 0], near_s)
    left_here(big_in.at[0, 0], whole_s)
    left_here(part_far.at[0, 0, :, pl.ds(0, 3), pl.ds(0, 3)], forward_s)
    left_here(big_in.at[0], cross_s.at[STEPS])


def shards(psi_start, diagonal, left_ops, right_ops, pair_in, pair_out, pair_count):
    vmem = pl.BlockSpec(memory_space=pltpu.VMEM)
    smem = pl.BlockSpec(memory_space=pltpu.SMEM)
    hbm = pl.BlockSpec(memory_space=pltpu.HBM)
    dma = pltpu.SemaphoreType.DMA
    rows = (3, 8, N)
    blocks = (4, 2, 2, *rows)
    pieces = (2, 3, 4, 4, 8, N)
    psi, energies = pl.pallas_call(
        kernel,
        out_shape=(
            jax.ShapeDtypeStruct(blocks, F32),
            jax.ShapeDtypeStruct((STEPS,), F32),
        ),
        in_specs=[hbm] * 7,
        out_specs=(vmem, smem),
        scratch_shapes=[
            pltpu.SMEM((1, 4), jnp.int32),
            pltpu.SMEM((1, 4), jnp.int32),
            pltpu.SMEM((1,), jnp.int32),
            pltpu.VMEM((8, N), F32),
            pltpu.VMEM((4, N, N), F32),
            pltpu.VMEM((4, N, N), F32),
            pltpu.VMEM((4, 2, N // 2, 3 * N), BF16),
            pltpu.VMEM((4, 3 * N, N), BF16),
            pltpu.VMEM((4, N, 3 * N), BF16),
            pltpu.VMEM((4, 3 * N, N), BF16),
            pltpu.VMEM((4, N // 2, N), F32),
            pltpu.VMEM((STEPS, 2, *pieces), F32),
            pltpu.VMEM((STEPS, *pieces), F32),
            pltpu.VMEM((STEPS, *pieces), F32),
            pltpu.VMEM((STEPS, *pieces), F32),
            pltpu.VMEM((STEPS, 2, 3, 3, 4, 8, N), F32),
            pltpu.VMEM((STEPS, 2, 3, 4, 8, N), F32),
            pltpu.VMEM((STEPS, 2, 3, 3, 8, N), F32),
            pltpu.VMEM((STEPS, 2, *rows), F32),
            pltpu.VMEM((STEPS, 7, 8, N), F32),
            pltpu.VMEM((STEPS + 1, 2, *rows), F32),
            pltpu.VMEM((STEPS, 18, 8, 128), F32),
            dma((19,)),
            dma,
            dma((3,)),
            dma,
            dma((3,)),
            dma,
            dma((3,)),
            dma((STEPS,)),
            dma((STEPS, 2, 3)),
            dma((STEPS,)),
            dma((STEPS, 2, 3)),
            dma((STEPS,)),
            dma((STEPS, 2, 3)),
            dma((STEPS,)),
            dma((STEPS,)),
            dma((STEPS,)),
            dma((STEPS, 3)),
            dma,
            dma((2, 3)),
            dma,
            dma((2, 3)),
            dma((STEPS + 1,)),
            dma((STEPS + 1,)),
            dma,
            dma((3,)),
            dma((STEPS,)),
            dma((STEPS, 4)),
        ],
        compiler_params=pltpu.CompilerParams(
            collective_id=0, has_side_effects=True, vmem_limit_bytes=60 * 1024 * 1024
        ),
    )(
        pair_in,
        pair_out,
        pair_count,
        psi_start.reshape(blocks),
        diagonal.reshape(blocks),
        left_ops,
        right_ops,
    )
    return psi.reshape(1, N, N), energies


def solution(mesh):
    both = ("term", "sector")
    in_specs = (
        P("sector", None, None),
        P("sector", None, None),
        P(both, None, None),
        P(both, None, None),
        P(both, None),
        P(both, None),
        P(both),
    )
    out_specs = (P("sector", None, None), P())
    return jax.shard_map(
        shards, mesh=mesh, in_specs=in_specs, out_specs=out_specs, check_vma=False
    )
```

time: 105 us -> 103 us (0.981)
  Pallas kernels: 100 us -> 98.9 us
    pallas_call x1, Pallas kernels: 100 us -> 98.9 us  [shards(): pl.pallas_call(kernel, out_shape=(jax.ShapeDtypeStruct(blocks, F32), jax....]
where the time goes in v4:
time: 103 us
  Pallas kernels  98.9 us (96%)
  local copies, waits for them, and re-layouts  3.09 us (3%)
  between operations  1.29 us (1%)
    pallas_call x1, Pallas kernels, shards(): pl.pallas_call(kernel, out_shape=(jax.ShapeDtypeStruct(blocks, F32), jax....  98.9 us
    unnamed x2, local copies, waits for them, and re-layouts  3.09 us

profile of v4, /device:TPU:1, one launch (start us, length us, event | category | flops | bytes accessed | tf_op | source)
XLA Modules:
  0.0 103.3 jit_solution(9164260341401262269)
XLA Ops:
  1.3 98.9 %shard_map.86 = (f32[4,2,2,3,8,384]{5,4,3,2,1,0:T(8,128)}, f32[2]{0:T(128)}) custom-call(s32[1,4]{1,0:T(1,128)} %pair_in_hbm.1, s32[1,4]{1,0:T(1,128)} %pair_out_hbm.1, s32[1]{0:T(128)S(6)} %copy.11.pair_count_hbm, f32[4,2,2,3,8,384]{5,4,3,2,1,0:T(8,128)} %bitcast.3, f32[4,2,2,3,8,384]{5,4,3,2,1,0:T(8,128)} %bitcast.4, f32[4,384,384]{2,1,0:T(8,128)} %left_hbm.1, ...), custom_call_target="tpu_custom_call" | custom-call | tf_op jit(solution)/shard_map/pallas_call | solution.py:494
  100.2 1.9 %copy.12 = f32[1,384,384]{2,1,0:T(8,128)} copy(f32[1,384,384]{2,1,0:T(8,128)} %bitcast.5) | data formatting | bytes 1179648
  102.1 1.2 %copy.13 = f32[2]{0:T(128)} copy(f32[2]{0:T(128)} %get-tuple-element.9) | data formatting | bytes 16

commit v5 on v4

--- a/solution.py
+++ b/solution.py
@@ -289,17 +289,24 @@
                     own[cls, b, p, q] = value + core_in[step, cls, b, p, q]
 
                 dot = combine(c, cls, b, store, dot)
+            return dot
+
+        def large(b):
+            if b:
+                left_here(big_in.at[0, :, 0], big_s.at[step, b - 1])
+            for cls in range(2):
                 for m in (2, 1, 3):
                     send(
                         own.at[cls, b, lax.rem(p_me[cls] + m, 4)],
                         big_in.at[step, cls, b, m - 1],
-                        big_s.at[step],
+                        big_s.at[step, b],
                         big_r.at[step, cls, b],
                         p_to[cls](m),
                     )
-            return dot
-
-        dot = lax.fori_loop(0, 3, near_rows, dot)
+
+        dot = near_rows(0, dot)
+        large(0)
+        dot = lax.fori_loop(1, 3, near_rows, dot)
 
         tiles = dots.at[step]
         tiles[c] = dot[:, 0:128] + dot[:, 128:256] + dot[:, 256:384]
@@ -371,12 +378,14 @@
             def _():
                 arrived(z_in.at[step, pl.ds(0, 2)], owner_r.at[step, b])
 
+        large(1)
         small(0)
         arrived(tiles.at[pl.ds(2, 7)], dot_r.at[step, 1])
         pairs = [tiles[2 + 2 * i] + tiles[3 + 2 * i] for i in range(4)]
         tiles[10 + x] = (pairs[0] + pairs[1]) + (pairs[2] + pairs[3])
         for k in (2, 1, 3):
             send(tiles.at[10 + x], tiles.at[10 + x], dot_s.at[step], dot_r.at[step, 2], x_to(k))
+        large(2)
         small(1)
         to_owner(0)
         arrived(tiles.at[pl.ds(10, 3)], dot_r.at[step, 2])
@@ -411,7 +420,7 @@
                     arrived(small_in.at[0, 0, 0], grow_r.at[cls, b])
                     here = after.at[c, cls, b, p_me[cls]]
                     for m in (2, 1, 3):
-                        send(here, here, wide_s, wide_r.at[cls, b], p_to[cls](m))
+                        send(here, here, wide_s.at[b], wide_r.at[cls, b], p_to[cls](m))
 
             def over(b):
                 for cls in range(2):
@@ -421,17 +430,18 @@
 
             grow(0)
             update(2, rayleigh)
+            grow(1)
             wide(0)
-            grow(1)
             grow(2)
             wide(1)
+            wide(2)
             over(0)
-            wide(2)
             over(1)
             over(2)
             arrived(after.at[d], cross_r.at[step])
             left_here(small_in.at[0], grow_s)
-            left_here(big_in.at[0], wide_s)
+            for b in range(3):
+                left_here(big_in.at[0, :, 0], wide_s.at[b])
             left_here(after.at[d], cross_s.at[step])
 
         @pl.when(step == STEPS - 1)
@@ -460,7 +470,7 @@
             left_here(out.at[:, d], cross_s.at[step])
 
         left_here(part_far.at[0], core_s.at[step])
-        left_here(big_in.at[0], big_s.at[step])
+        left_here(big_in.at[0, :, 0], big_s.at[step, 2])
         left_here(small_in.at[0], small_s.at[step])
         left_here(tiles.at[pl.ds(0, 14)], dot_s.at[step])
 
@@ -531,7 +541,7 @@
             dma((3,)),
             dma((STEPS,)),
             dma((STEPS, 2, 3)),
-            dma((STEPS,)),
+            dma((STEPS, 3)),
             dma((STEPS, 2, 3)),
             dma((STEPS,)),
             dma((STEPS, 2, 3)),
@@ -541,7 +551,7 @@
             dma((STEPS, 3)),
             dma,
             dma((2, 3)),
-            dma,
+            dma((3,)),
             dma((2, 3)),
             dma((STEPS + 1,)),
             dma((STEPS + 1,)),
@@ -551,7 +561,7 @@
             dma((STEPS, 4)),
         ],
         compiler_params=pltpu.CompilerParams(
-            collective_id=0, has_side_effects=True, vmem_limit_bytes=60 * 1024 * 1024
+            collective_id=0, has_side_effects=True, vmem_limit_bytes=54400 * 1024
         ),
     )(
         pair_in,

time: 103 us -> 101 us (0.981)
  Pallas kernels: 98.9 us -> 96.5 us
    pallas_call x1, Pallas kernels: 98.9 us -> 96.5 us  [shards(): pl.pallas_call(kernel, out_shape=(jax.ShapeDtypeStruct(blocks, F32), jax....]
    unnamed x2 -> x6, local copies, waits for them, and re-layouts: 3.09 us -> 2.63 us
where the time goes in v5:
time: 101 us; the launch traced here: 100 us
  Pallas kernels  96.5 us (96%)
  local copies, waits for them, and re-layouts  2.63 us (3%)
  between operations  1.3 us (1%)
    pallas_call x1, Pallas kernels, shards(): pl.pallas_call(kernel, out_shape=(jax.ShapeDtypeStruct(blocks, F32), jax....  96.5 us
    unnamed x6, local copies, waits for them, and re-layouts  2.63 us

profile of v5, /device:TPU:1, one launch (start us, length us, event | category | flops | bytes accessed | tf_op | source)
XLA Modules:
  0.0 100.4 jit_solution(4371527420890147280)
XLA Ops:
  1.3 0.0 copy-start
  1.3 0.6 copy-done
  1.9 0.0 copy-start.1
  1.9 0.7 copy-done.1
  2.6 96.5 %shard_map.86 = (f32[4,2,2,3,8,384]{5,4,3,2,1,0:T(8,128)S(1)}, f32[2]{0:T(128)S(1)}) custom-call(s32[1,4]{1,0:T(1,128)S(1)} %copy-done, s32[1,4]{1,0:T(1,128)S(1)} %copy-done.1, s32[1]{0:T(128)S(6)} %copy.11.pair_count_hbm, f32[4,2,2,3,8,384]{5,4,3,2,1,0:T(8,128)} %bitcast.4, f32[4,2,2,3,8,384]{5,4,3,2,1,0:T(8,128)} %bitcast.5, f32[4,384,384]{2,1,0:T(8,128)} %left_hbm.1, ...), custom_call_target="tpu_custom_call" | custom-call | tf_op jit(solution)/shard_map/pallas_call | solution.py:504
  99.1 0.8 copy.12
  99.9 0.5 copy.13
Async XLA Ops:
  1.3 0.7 copy-start
  1.9 0.7 copy-start.1

commit v6 on v5

--- a/solution.py
+++ b/solution.py
@@ -564,8 +564,8 @@
             collective_id=0, has_side_effects=True, vmem_limit_bytes=54400 * 1024
         ),
     )(
-        pair_in,
-        pair_out,
+        pltpu.with_memory_space_constraint(pair_in, pltpu.HBM),
+        pltpu.with_memory_space_constraint(pair_out, pltpu.HBM),
         pair_count,
         psi_start.reshape(blocks),
         diagonal.reshape(blocks),

time: 101 us -> 99.7 us (0.987)
  local copies, waits for them, and re-layouts: 2.63 us -> 1.33 us
    unnamed x6 -> x2, local copies, waits for them, and re-layouts: 2.63 us -> 1.33 us
where the time goes in v6:
time: 99.7 us; the launch traced here: 99.6 us
  Pallas kernels  97 us (97%)
  local copies, waits for them, and re-layouts  1.33 us (1%)
  between operations  1.29 us (1%)
    pallas_call x1, Pallas kernels, shards(): pl.pallas_call(kernel, out_shape=(jax.ShapeDtypeStruct(blocks, F32), jax....  97 us

profile of v6, /device:TPU:1, one launch (start us, length us, event | category | flops | bytes accessed | tf_op | source)
XLA Modules:
  0.0 99.6 jit_solution(1039165421192105357)
XLA Ops:
  1.3 97.0 %shard_map.86 = (f32[4,2,2,3,8,384]{5,4,3,2,1,0:T(8,128)S(1)}, f32[2]{0:T(128)S(1)}) custom-call(s32[1,4]{1,0:T(1,128)} %pair_in_hbm.1, s32[1,4]{1,0:T(1,128)} %pair_out_hbm.1, s32[1]{0:T(128)S(6)} %copy.11.pair_count_hbm, f32[4,2,2,3,8,384]{5,4,3,2,1,0:T(8,128)} %bitcast.4, f32[4,2,2,3,8,384]{5,4,3,2,1,0:T(8,128)} %bitcast.5, f32[4,384,384]{2,1,0:T(8,128)} %left_hbm.1, ...), custom_call_target="tpu_custom_call" | custom-call | tf_op jit(solution)/shard_map/pallas_call | solution.py:504
  98.2 0.8 copy.12
  99.1 0.5 copy.13

commit v7 on v6

--- a/solution.py
+++ b/solution.py
@@ -175,14 +175,15 @@
 
     lax.fori_loop(0, 4, split_right, 0)
 
-    def forward(k, carry):
+    def forward(i, carry):
+        k = lax.rem(2 * i, 3) + 1
         here = first.at[c, 0, :, x, lax.rem(y + 4 - k, 4)]
         arrived(here, near_r.at[k - 1])
         for m in (2, 1, 3):
             send(here, here, forward_s, forward_r.at[k - 1], x_to(m))
         return carry
 
-    lax.fori_loop(1, 4, forward, 0)
+    lax.fori_loop(0, 3, forward, 0)
 
     loads[1].wait()
 
@@ -202,7 +203,8 @@
     for load in loads[2:]:
         load.wait()
 
-    def cross(k, carry):
+    def cross(i, carry):
+        k = lax.rem(2 * i, 3) + 1
         sector = lax.rem(y + 4 - k, 4)
         arrived(small_in.at[0, 0], forward_r.at[k - 1])
         here = first.at[c, 0, :, :, sector]
@@ -212,7 +214,7 @@
         send(here, here, cross_s.at[STEPS], cross_r.at[STEPS], sibling)
         return carry
 
-    lax.fori_loop(1, 4, cross, 0)
+    lax.fori_loop(0, 3, cross, 0)
     arrived(big_in.at[0], cross_r.at[STEPS])
 
     count = pair_count[0]

time: 99.7 us -> 99.7 us (level)
  no operation moved by 1% of the time
where the time goes in v7:
time: 99.7 us; the launch traced here: 99.6 us
  Pallas kernels  97 us (97%)
  local copies, waits for them, and re-layouts  1.33 us (1%)
  between operations  1.29 us (1%)
    pallas_call x1, Pallas kernels, shards(): pl.pallas_call(kernel, out_shape=(jax.ShapeDtypeStruct(blocks, F32), jax....  97 us

profile of v7, /device:TPU:1, one launch (start us, length us, event | category | flops | bytes accessed | tf_op | source)
XLA Modules:
  0.0 99.6 jit_solution(17342903661022801057)
XLA Ops:
  1.3 97.0 %shard_map.86 = (f32[4,2,2,3,8,384]{5,4,3,2,1,0:T(8,128)S(1)}, f32[2]{0:T(128)S(1)}) custom-call(s32[1,4]{1,0:T(1,128)} %pair_in_hbm.1, s32[1,4]{1,0:T(1,128)} %pair_out_hbm.1, s32[1]{0:T(128)S(6)} %copy.11.pair_count_hbm, f32[4,2,2,3,8,384]{5,4,3,2,1,0:T(8,128)} %bitcast.4, f32[4,2,2,3,8,384]{5,4,3,2,1,0:T(8,128)} %bitcast.5, f32[4,384,384]{2,1,0:T(8,128)} %left_hbm.1, ...), custom_call_target="tpu_custom_call" | custom-call | tf_op jit(solution)/shard_map/pallas_call | solution.py:506
  98.3 0.8 copy.12
  99.1 0.5 copy.13
